TPU v7x, 128 devices: a whole 4x4x4 slice. The times are simulated.
128 devices in a mesh: dp: 16 (over x_lo, y, core), inner: 8 (over z, x_hi).
Axes of the slice: x: 4 (x_hi: 2, x_lo: 2; x = x_hi * 2 + x_lo), y: 4, z: 4, core: 2. Of those that a mesh axis runs over, the one named last changes fastest.
Arguments:
- features: bfloat16 [32768, 4096], P(('dp', 'inner')), may hold values from -6 to 6
- proj_weight: bfloat16 [4096, 128], replicated, may hold values from -0.09375 to 0.09375
- partner: int32 [32768], P(('dp', 'inner')), may hold values from 0 to 32767, as said below
Outputs:
- loss: float32 [], replicated
- grad_weight: float32 [4096, 128], replicated
Inputs may be any that keep to these rules, and one draw needn't show every extreme that they name: partner pairs the views: partner[partner[i]] == i and partner[i] != i; partners may lie on any device.
All inputs are finite; a program needn't handle non-finite values.
Results may differ from a plain program's by a relative error of at most 0.0006.
The roundings to bfloat16 on the way count: a program that leaves them out, or rounds other values in their place, can miss the bound.
Values may be sent and summed in bfloat16 or wider, within the bound.
A program may use at most 128 MiB of HBM per device.

v0:
```python
import math

import jax
import jax.numpy as jnp
from jax import lax
from jax.sharding import PartitionSpec as P


def per_device(features, proj_weight, partner):
    inv_tau = 5.0
    rows = features.shape[0]
    z = jnp.dot(features, proj_weight, preferred_element_type=jnp.float32)
    norm = jnp.sqrt(jnp.sum(z * z, axis=1, keepdims=True) + 1e-06)
    u = z / norm
    ub = u.astype(jnp.bfloat16)
    group = lax.all_gather(ub, "inner", axis=0, tiled=True)
    full = lax.all_gather(group, "dp", axis=0, tiled=True)
    views = full.shape[0]
    width = full.shape[1]
    first_own = (lax.axis_index("dp") * lax.axis_size("inner") + lax.axis_index("inner")) * rows
    own_ids = first_own + jnp.arange(rows, dtype=jnp.int32)
    block = math.gcd(4096, views)
    count = views // block

    def scores_at(first, length):
        columns = lax.dynamic_slice_in_dim(full, first, length, 0)
        scores = (
            lax.dot_general(
                ub, columns, (((1,), (1,)), ((), ())), preferred_element_type=jnp.float32
            )
            * inv_tau
        )
        mask = own_ids[:, None] == (first + jnp.arange(length, dtype=jnp.int32))[None, :]
        return (scores, mask, columns)

    def add_sums(step, total):
        scores, mask, columns = scores_at(step * block, block)
        expo = jnp.where(mask, jnp.float32(0.0), jnp.exp(scores - inv_tau))
        return total + jnp.sum(expo, axis=1)

    rowsum = lax.fori_loop(0, count, add_sums, jnp.zeros((rows,), jnp.float32))
    lse = inv_tau + jnp.log(rowsum)
    paired = full[partner]
    pos = jnp.sum(ub.astype(jnp.float32) * paired.astype(jnp.float32), axis=1) * inv_tau
    loss_part = jnp.sum(lse - pos)

    def add_rows(step, total):
        scores, mask, columns = scores_at(step * block, block)
        probs = jnp.where(mask, jnp.float32(0.0), jnp.exp(scores - lse[:, None])).astype(
            jnp.bfloat16
        )
        return total + jnp.dot(probs, columns, preferred_element_type=jnp.float32)

    row_term = lax.fori_loop(0, count, add_rows, jnp.zeros((rows, width), jnp.float32))
    scores, mask, columns = scores_at(jnp.int32(0), lax.axis_size(("dp", "inner")) * rows)
    probs = jnp.where(mask, jnp.float32(0.0), jnp.exp(scores - lse[:, None])).astype(jnp.bfloat16)
    col_term = lax.psum_scatter(
        lax.dot_general(probs, ub, (((0,), (0,)), ((), ())), preferred_element_type=jnp.float32),
        ("dp", "inner"),
        scatter_dimension=0,
        tiled=True,
    )
    terms = row_term + col_term
    du = inv_tau * (terms - 2.0 * paired.astype(jnp.float32))
    dz = ((du - u * jnp.sum(u * du, axis=1, keepdims=True)) / norm).astype(jnp.bfloat16)
    grad_part = lax.dot_general(
        features, dz, (((0,), (0,)), ((), ())), preferred_element_type=jnp.float32
    )
    loss_total, grad_total = lax.psum((loss_part, grad_part), ("dp", "inner"))
    return (loss_total / views, grad_total / jnp.sqrt(jnp.float32(views)))


def solution(mesh):
    placed = (P(("dp", "inner"), None), P(), P(("dp", "inner")))
    return jax.shard_map(
        per_device, mesh=mesh, in_specs=placed, out_specs=(P(), P()), check_vma=False
    )
```

profile of v0, /device:TPU:1, one launch (start us, length us, event | category | flops | bytes accessed | tf_op | source)
XLA Modules:
  0.0 1012.5 jit_solution(16293020059966114238)
XLA Ops:
  7.2 1.5 copy-done
  8.8 2.1 multiply_reduce_fusion.1
  10.9 34.8 %all_gather.6 = bf16[2048,128]{0,1:T(8,128)(2,1)} all-gather(bf16[256,128]{0,1:T(8,128)(2,1)S(1)} %fusion.39), channel_id=1, replica_groups=mesh['dp'=16,'inner'=8] {'inner'}, dimensions={0}, use_global_device_ids=true | all-gather | bytes 589824 | tf_op jit(solution)/shard_map/all_gather | solution.py:16
  45.9 58.9 %all-gather.2.cloned.1.call-done = bf16[32768,128]{0,1:T(8,128)(2,1)} async-done(((bf16[2048,128]{0,1:T(8,128)(2,1)}), bf16[32768,128]{0,1:T(8,128)(2,1)}) %all-gather.2.cloned.1.call-update) | async-done | bytes 8388624 | tf_op jit(solution)/shard_map/all_gather | solution.py:17
  104.8 11.9 %copy.5 = bf16[32768,128]{1,0:T(8,128)(2,1)} copy(bf16[32768,128]{0,1:T(8,128)(2,1)} %all-gather.2.cloned.1.call-done) | data formatting | bytes 16777216
  116.7 19.6 %while.30 = (s32[]{:T(128)}, f32[256]{0:T(256)S(1)}, bf16[32768,128]{1,0:T(8,128)(2,1)}, bf16[256,128]{1,0:T(8,128)(2,1)S(1)}, s32[]{:T(128)}, /*index=5*/s32[]{:T(128)}, s32[]{:T(128)}, s32[]{:T(128)}, s32[]{:T(128)}) while((s32[]{:T(128)}, f32[256]{0:T(256)S(1)}, bf16[32768,128]{1,0:T(8,128)(2,1)}, ...), condition=%wide.region_3.4_spmd.clone, body=%wide.region_1.3_spmd.clone.sunk | while | flops 273682944 | bytes 1153193 | solution.py:41
  116.7 2.4 fusion.57
  119.2 2.4 fusion.57
  121.6 2.4 fusion.57
  124.1 2.4 fusion.57
  126.5 2.4 fusion.57
  129.0 2.4 fusion.57
  131.5 2.4 fusion.57
  133.9 2.4 fusion.57
  136.4 15.7 %fusion.28 = f32[32768,128]{0,1:T(8,128)} fusion(bf16[256,128]{0,1:T(8,128)(2,1)S(1)} %fusion.39, bf16[32768,128]{0,1:T(8,128)(2,1)} %all-gather.2.cloned.1.call-done, f32[256]{0:T(256)S(1)} %log_add_fusion, s32[256]{0:T(256)S(1)} %iota_add_fusion.4), kind=kOutput, calls=%fused_computation.34 | convolution fusion | flops 4336910336 | bytes 25233408 | tf_op jit(solution)/shard_map/dot_general | solution.py:58
  152.7 24.4 %while.31 = (s32[]{:T(128)}, f32[256,128]{1,0:T(8,128)S(1)}, bf16[32768,128]{1,0:T(8,128)(2,1)}, bf16[256,128]{1,0:T(8,128)(2,1)S(1)}, f32[256]{0:T(256)S(1)}, /...) while((s32[]{:T(128)}, f32[256,128]{1,0:T(8,128)S(1)}, ...), condition=%wide.region_8.9_spmd.clone, body=%wide.region_7.8_spmd.clone.sunk | while | flops 542183680 | bytes 2462380 | solution.py:54
  152.8 3.1 fusion.61
  155.9 3.0 fusion.61
  158.9 3.0 fusion.61
  162.0 3.0 fusion.61
  165.0 3.0 fusion.61
  168.0 3.0 fusion.61
  171.1 3.0 fusion.61
  174.1 3.0 fusion.61
  177.2 5.2 gather_fusion
  182.6 654.3 %reduce-scatter.2.cloned.1.call-done = f32[256,128]{0,1:T(8,128)} async-done(((f32[32768,128]{0,1:T(8,128)}), f32[256,128]{0,1:T(8,128)}) %reduce-scatter.2.cloned.1.call-update) | async-done | bytes 131088 | tf_op jit(solution)/shard_map/reduce_scatter | solution.py:57
  836.9 1.0 multiply_reduce_fusion
  837.9 2.7 convolution_bitcast_fusion
  841.2 72.8 %psum.14 = f32[]{:T(128)} all-reduce(f32[]{:T(128)} %subtract_reduce_fusion), channel_id=1, replica_groups=mesh['dp'=16,'inner'=8] {'dp','inner'}, use_global_device_ids=true, to_apply=%region_6.7 | all-reduce | flops 1 | bytes 8 | tf_op jit(solution)/shard_map/psum | solution.py:69
  914.6 84.2 %all-reduce.2.cloned.1.call-done = f32[4096,128]{0,1:T(8,128)} async-done(((f32[4096,128]{0,1:T(8,128)}), f32[4096,128]{0,1:T(8,128)}) %all-reduce.2.cloned.1.call-update) | async-done | bytes 2097168 | tf_op jit(solution)/shard_map/psum | solution.py:69
  998.9 3.1 broadcast_multiply_fusion
  1002.0 2.9 copy.13
  (61 shorter events, 2.0 us)
Async XLA Ops:
  7.2 1.6 copy-start
  7.2 97.6 %all-gather.2.cloned.1.call-start = ((), (), s32[]{:S(2)}) async-start(), calls=%async_computation.1 | async-start | bytes 8912896 | tf_op jit(solution)/shard_map/all_gather | solution.py:17
  45.7 791.2 %reduce-scatter.2.cloned.1.call-start = ((), (), s32[]{:S(2)}) async-start(), calls=%async_computation.2 | async-start | bytes 16908288 | tf_op jit(solution)/shard_map/reduce_scatter | solution.py:57
  152.1 0.7 copy-start.1
  152.1 846.8 %all-reduce.2.cloned.1.call-start = ((), (), s32[]{:S(2)}) async-start(), calls=%async_computation.3 | async-start | bytes 4194304 | tf_op jit(solution)/shard_map/psum | solution.py:69
Sparse Core Ops, SparseCore 0:
  45.8 58.9 all-gather.1
  152.2 684.6 reduce-scatter.1
  842.3 156.4 all-reduce.1
where the time goes:
time: 1010 us
  waiting for transfers between devices  797 us (79%)
  blocking collectives  108 us (11%)
  matrix products  63.5 us (6%)
  local copies, waits for them, and re-layouts  22.5 us (2%)
  between operations  15.6 us (2%)
    reduce_scatter x1, waiting for transfers between devices, per_device(): lax.psum_scatter(lax.dot_general(probs, ub, (((0,), (0,)), ((), ())), pre...  654 us
    psum x1, waiting for transfers between devices, per_device(): loss_total, grad_total = lax.psum((loss_part, grad_part), ('dp', 'inner'))  84.2 us
    psum x1, blocking collectives, per_device(): loss_total, grad_total = lax.psum((loss_part, grad_part), ('dp', 'inner'))  72.8 us
    all_gather x1, waiting for transfers between devices, per_device(): full = lax.all_gather(group, 'dp', axis=0, tiled=True)  58.9 us
    all_gather x1, blocking collectives, per_device(): group = lax.all_gather(ub, 'inner', axis=0, tiled=True)  34.8 us
    dot_general x8, matrix products, add_rows(): return total + jnp.dot(probs, columns, preferred_element_type=jnp.float32)  23.9 us
  transfers between devices with their start and end apart: 3, of which 3 were waited for; matrix products, arithmetic and copies ran while one was open for 3% of the time, Pallas kernels for 0%

commit v1 on v0

v1 whole, which is shorter than its diff:
```python
import jax
import jax.numpy as jnp
from jax import lax
from jax.experimental import pallas as pl
from jax.experimental.pallas import tpu as pltpu
from jax.sharding import PartitionSpec as P

MESH = pl.DeviceIdType.MESH
F32 = jnp.float32
BF16 = jnp.bfloat16
VIEWS = 32768
D = 4096
HALF = D // 2
PROJ = 128
OWN = 256
SLOT = OWN + 16
INV_TAU = 5.0
SCALE2 = INV_TAU * 1.4426950408889634
NT = (((1,), (1,)), ((), ()))
TN = (((0,), (0,)), ((), ()))
EXACT = lax.Precision.HIGHEST

ROW_OFFS = [(dx, dc) for dc in range(2) for dx in range(4)]
ROW_OF = {off: slot for slot, off in enumerate(ROW_OFFS)}
COL_OFFS = sorted(
    [(dy, dz) for dy in range(4) for dz in range(4)],
    key=lambda o: (min(o[0], 4 - o[0]) + min(o[1], 4 - o[1]), o),
)
COL_OF = {off: slot for slot, off in enumerate(COL_OFFS)}
PARTS = ("x", "y", "z", "m")
PART_ROWS = HALF // len(PARTS)
RING_ROWS = PART_ROWS // 4
TILE = RING_ROWS // 16


def neg_col(off):
    return ((-off[0]) % 4, (-off[1]) % 4)


def neg_row(off):
    return ((-off[0]) % 4, off[1])


def coords():
    dp, inner = lax.axis_index("dp"), lax.axis_index("inner")
    x = (inner % 2) * 2 + dp // 8
    return x, (dp // 2) % 4, inner // 2, dp % 2


def device_at(x, y, z, c):
    return ((x % 2) * 8 + y * 2 + c, z * 2 + x // 2)


def peer(dx=0, dy=0, dz=0, dc=0):
    x, y, z, c = coords()
    return device_at((x + dx) % 4, (y + dy) % 4, (z + dz) % 4, (c + dc) % 2)


def ring_peer(part, d):
    c = coords()[3]
    if part == "x":
        return peer(dx=d)
    if part == "y":
        return peer(dy=d)
    if part == "z":
        return peer(dz=d)
    return peer(dx=d * (1 - c), dy=d * c)


def plane_peer(part, d1, d2):
    c = coords()[3]
    if part == "x":
        return peer(dy=d1, dz=d2)
    if part == "y":
        return peer(dx=d1, dz=d2)
    if part == "z":
        return peer(dx=d1, dy=d2)
    return peer(dx=d1 * c, dy=d1 * (1 - c), dz=d2)


def part_place(part):
    x, y, z, c = coords()
    if part == "x":
        return x, y, z
    if part == "y":
        return y, x, z
    if part == "z":
        return z, x, y
    return x * (1 - c) + y * c, y * (1 - c) + x * c, z


def all_peers():
    offs = []
    for dx in range(4):
        for dy in range(4):
            for dz in range(4):
                if (dx, dy, dz) != (0, 0, 0) and 0 in (dx, dy, dz):
                    offs.append((dx, dy, dz, 0))
    offs += [(dx, 0, 0, 1) for dx in range(4)]
    return offs


def send(src, dst, send_sem, recv_sem, device):
    copy = pltpu.make_async_remote_copy(
        src_ref=src, dst_ref=dst, send_sem=send_sem, recv_sem=recv_sem,
        device_id=device, device_id_type=MESH,
    )
    copy.start()


def wait_bytes(ref, sem):
    pltpu.make_async_copy(ref, ref, sem).wait()


def kernel(
    f_hbm, w_hbm, code_ref, g_hbm, loss_ref,
    feat, weight, feat_sib, u_ref, norm_ref, rows, cols, expo, acc,
    sums, sums_in, wts, wts_in, wide, paired, uw, quad, quad_sib, quad_ring,
    dz_own, dz_sib, grad, g1_in, g1, g2_in, out, loss1, loss2,
    load_sem, x_send, col_recv, row_recv, feat_recv, sum_recv, wt_recv, loss_recv1, loss_recv2,
    qs_recv, qr_recv, dz_recv, g1_recv, g2_recv, ag_recv, ring_recv, rel_recv, store_sem,
):
    x, y, z, c = coords()
    barrier = pltpu.get_barrier_semaphore()
    peers = all_peers()
    for off in peers:
        pl.semaphore_signal(barrier, inc=1, device_id=peer(*off), device_id_type=MESH)
    load_w = pltpu.make_async_copy(w_hbm, weight, load_sem.at[0])
    load_f = pltpu.make_async_copy(f_hbm, feat, load_sem.at[1])
    load_w.start()
    load_f.start()
    load_w.wait()
    load_f.wait()

    zed = jnp.dot(feat[...], weight[...], preferred_element_type=F32)
    norm = jnp.sqrt(jnp.sum(zed * zed, axis=1, keepdims=True) + 1e-06)
    u = zed / norm
    u_ref[...] = u
    norm_ref[...] = jnp.broadcast_to(norm, (OWN, PROJ))
    ub = u.astype(BF16)
    rows[0:OWN, :] = ub
    rows[OWN:SLOT, :] = code_ref[...]
    cols[0:OWN, :] = ub
    pl.semaphore_wait(barrier, len(peers))

    def row_slot(slot):
        return rows.at[pl.ds(slot * SLOT, SLOT)]

    def col_slot(slot):
        return cols.at[pl.ds(slot * OWN, OWN)]

    for dx in (2, 1, 3):
        to = ROW_OF[neg_row((dx, 0))]
        send(row_slot(0), row_slot(to), x_send.at[0], row_recv.at[to], peer(dx=dx))
    send(row_slot(0), row_slot(4), x_send.at[0], row_recv.at[4], peer(dc=1))
    for slot in range(1, 16):
        dy, dz = COL_OFFS[slot]
        to = COL_OF[neg_col((dy, dz))]
        send(col_slot(0), col_slot(to), x_send.at[1], col_recv.at[to], peer(dy=dy, dz=dz))
    send(
        feat.at[:, pl.ds(pl.multiple_of((1 - c) * HALF, HALF), HALF)], feat_sib,
        x_send.at[2], feat_recv.at[0], peer(dc=1),
    )

    def lanes(e):
        total = e[:, 0:PROJ]
        for q in range(1, e.shape[1] // PROJ):
            total = total + e[:, q * PROJ : (q + 1) * PROJ]
        return total

    def scores(slot, first):
        return jnp.exp2(
            lax.dot_general(
                rows[slot * SLOT : slot * SLOT + OWN, :], cols[pl.ds(first, OWN), :], NT,
                preferred_element_type=F32,
            )
            * SCALE2
        )

    for slot in (0, 4, 1, 3, 2, 5, 7, 6):
        if slot:
            wait_bytes(row_slot(slot), row_recv.at[slot])
        if slot in (1, 2, 3):
            send(row_slot(slot), row_slot(4 + slot), x_send.at[0], row_recv.at[4 + slot], peer(dc=1))
        e = scores(slot, 0)
        if slot == 0:
            at_row = lax.broadcasted_iota(jnp.int32, (OWN, OWN), 0)
            at_col = lax.broadcasted_iota(jnp.int32, (OWN, OWN), 1)
            e = jnp.where(at_row == at_col, 0.0, e)
        expo[slot * OWN : (slot + 1) * OWN, 0:OWN] = e.astype(BF16)
        acc[slot * OWN : (slot + 1) * OWN, :] = lanes(e)

    def pass1(step, carry):
        first = pl.multiple_of(step * OWN, OWN)
        wait_bytes(cols.at[pl.ds(first, OWN)], col_recv.at[step])
        for slot in range(8):
            e = scores(slot, first)
            expo[slot * OWN : (slot + 1) * OWN, pl.ds(first, OWN)] = e.astype(BF16)
            acc[slot * OWN : (slot + 1) * OWN, :] += lanes(e)
        return carry

    lax.fori_loop(1, 16, pass1, 0)

    ones = jnp.ones((8, PROJ), F32)
    for slot in range(8):
        part = lax.dot_general(
            ones, acc[slot * OWN : (slot + 1) * OWN, :], NT,
            preferred_element_type=F32, precision=EXACT,
        )
        sums[slot : slot + 1, :] = part[0:1, :]
    for slot in (2, 6, 1, 3, 5, 7, 4):
        dx, dc = ROW_OFFS[slot]
        to = ROW_OF[neg_row((dx, dc))]
        send(sums, sums_in.at[to], x_send.at[3], sum_recv.at[to], peer(dx=dx, dc=dc))

    for slot in range(16):
        wide[:, slot * PROJ : (slot + 1) * PROJ] = cols[slot * OWN : (slot + 1) * OWN, :]
    sel_row = lax.broadcasted_iota(jnp.int32, (16, PROJ), 0)
    lane = lax.broadcasted_iota(jnp.int32, (OWN, PROJ), 1).astype(F32)

    def column_of(code, at):
        halves = [
            lax.dot_general(
                code, jnp.where(sel_row == at + h, 1.0, 0.0).astype(BF16), TN,
                preferred_element_type=F32,
            )
            for h in range(2)
        ]
        return jnp.concatenate(halves, axis=0)

    def partners(slot, pos):
        code = rows[slot * SLOT + OWN : (slot + 1) * SLOT, :]
        owner, place = column_of(code, 0), column_of(code, 2)
        hot = jnp.concatenate(
            [jnp.where(place == lane, 1.0, 0.0), jnp.where(place == lane + PROJ, 1.0, 0.0)], axis=1
        ).astype(BF16)
        found = jnp.dot(hot, wide[...], preferred_element_type=F32)
        total = jnp.zeros((OWN, PROJ), F32)
        for k in range(16):
            dy, dz = COL_OFFS[k]
            dp, inner = peer(dy=dy, dz=dz)
            here = (dp * 8 + inner).astype(F32)
            total = total + jnp.where(owner == here, found[:, k * PROJ : (k + 1) * PROJ], 0.0)
        paired[slot * OWN : (slot + 1) * OWN, :] = total
        own = rows[slot * SLOT : slot * SLOT + OWN, :].astype(F32)
        return pos + own * total

    pos = jnp.zeros((OWN, PROJ), F32)
    for slot in range(4):
        pos = partners(slot, pos)

    for slot in range(1, 8):
        wait_bytes(sums_in.at[slot], sum_recv.at[slot])
    for slot in range(8):
        dx, dc = ROW_OFFS[slot]
        total = sums[slot : slot + 1, :]
        for sender in range(1, 8):
            ox, oc = ROW_OFFS[sender]
            at = ROW_OF[((dx - ox) % 4, (dc - oc) % 2)]
            total = total + sums_in[sender, at : at + 1, :]
        wts[slot : slot + 1, :] = 1.0 / total
        if slot == 0:
            log_sum = jnp.sum(jnp.log(total))
    for slot in range(1, 16):
        dy, dz = COL_OFFS[slot]
        to = COL_OF[neg_col((dy, dz))]
        send(wts, wts_in.at[to], x_send.at[4], wt_recv.at[to], peer(dy=dy, dz=dz))

    for slot in range(4, 8):
        pos = partners(slot, pos)
    loss_part = log_sum - INV_TAU * jnp.sum(pos)
    me1 = x * 2 + c
    loss1[me1] = jnp.full((8, PROJ), loss_part, F32)
    for slot in range(1, 8):
        dx, dc = ROW_OFFS[slot]
        to = ROW_OF[neg_row((dx, dc))]
        send(loss1.at[me1], loss1.at[me1], x_send.at[5], loss_recv1.at[to], peer(dx=dx, dc=dc))

    sel8 = jnp.where(lax.broadcasted_iota(jnp.int32, (8, PROJ), 0) == 0, 1.0, 0.0)

    def weigh(slot, table):
        w = lax.dot_general(table, sel8, TN, preferred_element_type=F32, precision=EXACT)
        block = cols[slot * OWN : (slot + 1) * OWN, :]
        uw[slot * OWN : (slot + 1) * OWN, 0:PROJ] = block
        uw[slot * OWN : (slot + 1) * OWN, PROJ : 2 * PROJ] = (block.astype(F32) * w).astype(BF16)

    weigh(0, wts[...])
    for slot in range(1, 16):
        wait_bytes(wts_in.at[slot], wt_recv.at[slot])
        weigh(slot, wts_in[slot])

    def terms(slot):
        both = jnp.dot(
            expo[slot * OWN : (slot + 1) * OWN, :], uw[...], preferred_element_type=F32
        )
        sel = jnp.where(lax.broadcasted_iota(jnp.int32, (8, PROJ), 0) == slot, 1.0, 0.0)
        w = lax.dot_general(wts[...], sel, TN, preferred_element_type=F32, precision=EXACT)
        return (
            w * both[:, 0:PROJ] + both[:, PROJ : 2 * PROJ]
            - 2.0 * paired[slot * OWN : (slot + 1) * OWN, :]
        )

    def quad_slot(slot):
        return quad.at[pl.ds(slot * OWN, OWN)]

    for slot in (6, 5, 7, 4):
        quad[slot * OWN : (slot + 1) * OWN, :] = terms(slot)
        send(quad_slot(slot), quad_sib.at[slot - 4], x_send.at[6], qs_recv.at[slot - 4], peer(dc=1))
    for slot in (2, 1, 3, 0):
        part = terms(slot)
        wait_bytes(quad_sib.at[slot], qs_recv.at[slot])
        quad[slot * OWN : (slot + 1) * OWN, :] = part + quad_sib[slot]
        if slot:
            to = (-slot) % 4
            send(quad_slot(slot), quad_ring.at[to], x_send.at[7], qr_recv.at[to], peer(dx=slot))

    for slot in range(1, 8):
        wait_bytes(loss1.at[0], loss_recv1.at[slot])
    total = loss1[0]
    for k in range(1, 8):
        total = total + loss1[k]
    me2 = y * 4 + z
    loss2[me2] = total
    for slot in range(1, 16):
        dy, dz = COL_OFFS[slot]
        to = COL_OF[neg_col((dy, dz))]
        send(loss2.at[me2], loss2.at[me2], x_send.at[8], loss_recv2.at[to], peer(dy=dy, dz=dz))

    summed = quad[0:OWN, :]
    for d in (1, 3, 2):
        wait_bytes(quad_ring.at[d], qr_recv.at[d])
        summed = summed + quad_ring[d]
    du = INV_TAU * summed
    uu = u_ref[...]
    dz_own[...] = (
        (du - uu * jnp.sum(uu * du, axis=1, keepdims=True)) / norm_ref[...]
    ).astype(BF16)
    send(dz_own, dz_sib, x_send.at[9], dz_recv.at[0], peer(dc=1))

    mine = pl.multiple_of(c * HALF, HALF)
    grad[...] = lax.dot_general(
        feat[:, pl.ds(mine, HALF)], dz_own[...], TN, preferred_element_type=F32
    )
    wait_bytes(feat_sib, feat_recv.at[0])
    wait_bytes(dz_sib, dz_recv.at[0])
    grad[...] += lax.dot_general(feat_sib[...], dz_sib[...], TN, preferred_element_type=F32)

    def ring_block(part, t):
        return pl.ds(pl.multiple_of(part * PART_ROWS + t * RING_ROWS, RING_ROWS), RING_ROWS)

    places = [part_place(name) for name in PARTS]
    for d in (2, 1, 3):
        for p, name in enumerate(PARTS):
            t = places[p][0]
            at = (-d) % 4
            send(
                grad.at[ring_block(p, (t + d) % 4)], g1_in.at[p, at],
                x_send.at[10], g1_recv.at[p, at], ring_peer(name, d),
            )
    for p, name in enumerate(PARTS):
        t, s1, s2 = places[p]
        total = grad[ring_block(p, t), :]
        for d in range(1, 4):
            wait_bytes(g1_in.at[p, d], g1_recv.at[p, d])
            total = total + g1_in[p, d]
        g1[p] = total
        for slot in range(15, 0, -1):
            d1, d2 = COL_OFFS[slot]
            to = COL_OF[neg_col((d1, d2))]
            at = ((s1 + d1) % 4) * 4 + (s2 + d2) % 4
            send(
                g1.at[p, pl.ds(pl.multiple_of(at * TILE, TILE), TILE)],
                g2_in.at[p, pl.ds(to * TILE, TILE)],
                x_send.at[11], g2_recv.at[p], plane_peer(name, d1, d2),
            )
    base = c * HALF
    for p, name in enumerate(PARTS):
        t, s1, s2 = places[p]
        total = g1[p, pl.ds(pl.multiple_of((s1 * 4 + s2) * TILE, TILE), TILE), :]
        wait_bytes(g2_in.at[p, pl.ds(TILE, 15 * TILE)], g2_recv.at[p])
        for slot in range(1, 16):
            total = total + g2_in[p, slot * TILE : (slot + 1) * TILE, :]
        at = pl.ds(
            pl.multiple_of(base + p * PART_ROWS + t * RING_ROWS + (s1 * 4 + s2) * TILE, TILE), TILE
        )
        out[at, :] = total * (1.0 / VIEWS**0.5)
        for slot in range(15, 0, -1):
            d1, d2 = COL_OFFS[slot]
            send(out.at[at], out.at[at], x_send.at[12], ag_recv.at[p], plane_peer(name, d1, d2))

    def out_block(p, t, first=base):
        return out.at[
            pl.ds(pl.multiple_of(first + p * PART_ROWS + t * RING_ROWS, RING_ROWS), RING_ROWS)
        ]

    for p, name in enumerate(PARTS):
        t = places[p][0]
        wait_bytes(out.at[pl.ds(0, 15 * TILE)], ag_recv.at[p])
        block = out_block(p, t)
        for d in (2, 1, 3):
            at = (-d) % 4
            send(block, block, x_send.at[13], ring_recv.at[p, at], ring_peer(name, d))
        send(block, block, x_send.at[14], rel_recv.at[p, 0], peer(dc=1))
    for d in (1, 3, 2):
        for p, name in enumerate(PARTS):
            t = places[p][0]
            block = out_block(p, (t + d) % 4)
            wait_bytes(block, ring_recv.at[p, d])
            send(block, block, x_send.at[14], rel_recv.at[p, d], peer(dc=1))
    half = out.at[pl.ds(pl.multiple_of(base, HALF), HALF)]
    store1 = pltpu.make_async_copy(
        half, g_hbm.at[pl.ds(pl.multiple_of(base, HALF), HALF)], store_sem.at[0]
    )
    store1.start()

    for slot in range(1, 16):
        wait_bytes(loss2.at[0], loss_recv2.at[slot])
    total = loss2[0]
    for k in range(1, 16):
        total = total + loss2[k]
    loss_ref[...] = total * (1.0 / VIEWS)

    for d in (0, 1, 3, 2):
        for p in range(len(PARTS)):
            wait_bytes(out.at[pl.ds(0, RING_ROWS)], rel_recv.at[p, d])
    other = pl.multiple_of((1 - c) * HALF, HALF)
    store2 = pltpu.make_async_copy(
        out.at[pl.ds(other, HALF)], g_hbm.at[pl.ds(other, HALF)], store_sem.at[1]
    )
    store2.start()

    wait_bytes(rows.at[pl.ds(0, 7 * SLOT)], x_send.at[0])
    wait_bytes(cols.at[pl.ds(0, 15 * OWN)], x_send.at[1])
    wait_bytes(feat_sib, x_send.at[2])
    wait_bytes(sums_in.at[pl.ds(0, 7)], x_send.at[3])
    wait_bytes(wts_in.at[pl.ds(0, 15)], x_send.at[4])
    wait_bytes(loss1.at[pl.ds(0, 7)], x_send.at[5])
    wait_bytes(quad_sib, x_send.at[6])
    wait_bytes(quad_ring.at[pl.ds(0, 3)], x_send.at[7])
    wait_bytes(loss2.at[pl.ds(0, 15)], x_send.at[8])
    wait_bytes(dz_sib, x_send.at[9])
    wait_bytes(grad.at[pl.ds(0, 12 * RING_ROWS)], x_send.at[10])
    wait_bytes(grad.at[pl.ds(0, 60 * TILE)], x_send.at[11])
    wait_bytes(grad.at[pl.ds(0, 60 * TILE)], x_send.at[12])
    wait_bytes(grad.at[pl.ds(0, 12 * RING_ROWS)], x_send.at[13])
    wait_bytes(grad, x_send.at[14])
    store1.wait()
    store2.wait()


def per_device(features, proj_weight, partner):
    code = jnp.concatenate([partner // OWN, partner % OWN]).reshape(4, PROJ)
    code = jnp.pad(code, ((0, 12), (0, 0))).astype(BF16)
    dma = pltpu.SemaphoreType.DMA
    grad, loss = pl.pallas_call(
        kernel,
        out_shape=(
            jax.ShapeDtypeStruct((D, PROJ), F32),
            jax.ShapeDtypeStruct((8, PROJ), F32),
        ),
        in_specs=[
            pl.BlockSpec(memory_space=pl.ANY),
            pl.BlockSpec(memory_space=pl.ANY),
            pl.BlockSpec(memory_space=pltpu.VMEM),
        ],
        out_specs=(pl.BlockSpec(memory_space=pl.ANY), pl.BlockSpec(memory_space=pltpu.VMEM)),
        scratch_shapes=[
            pltpu.VMEM((OWN, D), BF16),
            pltpu.VMEM((D, PROJ), BF16),
            pltpu.VMEM((OWN, HALF), BF16),
            pltpu.VMEM((OWN, PROJ), F32),
            pltpu.VMEM((OWN, PROJ), F32),
            pltpu.VMEM((8 * SLOT, PROJ), BF16),
            pltpu.VMEM((16 * OWN, PROJ), BF16),
            pltpu.VMEM((8 * OWN, 16 * OWN), BF16),
            pltpu.VMEM((8 * OWN, PROJ), F32),
            pltpu.VMEM((8, OWN), F32),
            pltpu.VMEM((8, 8, OWN), F32),
            pltpu.VMEM((8, OWN), F32),
            pltpu.VMEM((16, 8, OWN), F32),
            pltpu.VMEM((OWN, 16 * PROJ), BF16),
            pltpu.VMEM((8 * OWN, PROJ), F32),
            pltpu.VMEM((16 * OWN, 2 * PROJ), BF16),
            pltpu.VMEM((8 * OWN, PROJ), F32),
            pltpu.VMEM((4, OWN, PROJ), F32),
            pltpu.VMEM((4, OWN, PROJ), F32),
            pltpu.VMEM((OWN, PROJ), BF16),
            pltpu.VMEM((OWN, PROJ), BF16),
            pltpu.VMEM((HALF, PROJ), F32),
            pltpu.VMEM((4, 4, RING_ROWS, PROJ), F32),
            pltpu.VMEM((4, RING_ROWS, PROJ), F32),
            pltpu.VMEM((4, RING_ROWS, PROJ), F32),
            pltpu.VMEM((D, PROJ), F32),
            pltpu.VMEM((8, 8, PROJ), F32),
            pltpu.VMEM((16, 8, PROJ), F32),
            dma((2,)),
            dma((15,)),
            dma((16,)),
            dma((8,)),
            dma((1,)),
            dma((8,)),
            dma((16,)),
            dma((8,)),
            dma((16,)),
            dma((4,)),
            dma((4,)),
            dma((1,)),
            dma((4, 4)),
            dma((4,)),
            dma((4,)),
            dma((4, 4)),
            dma((4, 4)),
            dma((2,)),
        ],
        compiler_params=pltpu.CompilerParams(
            collective_id=0, has_side_effects=True, vmem_limit_bytes=56 * 2**20
        ),
        name="simclr_head",
    )(features, proj_weight, code)
    return loss[0, 0], grad


def solution(mesh):
    placed = (P(("dp", "inner"), None), P(), P(("dp", "inner")))
    return jax.shard_map(
        per_device, mesh=mesh, in_specs=placed, out_specs=(P(), P()), check_vma=False
    )
```

time: 1010 us -> 89.5 us (0.09)
  waiting for transfers between devices: 797 us -> 0 us
  blocking collectives: 108 us -> 0 us
  Pallas kernels: 0 us -> 83.1 us
  matrix products: 63.5 us -> 0 us
  local copies, waits for them, and re-layouts: 22.5 us -> 4.24 us
  between operations: 15.6 us -> 0.64 us
    reduce_scatter x1 -> x0, waiting for transfers between devices: 654 us -> none  [per_device(): lax.psum_scatter(lax.dot_general(probs, ub, (((0,), (0,)), ((), ())), pre...]
    psum x1 -> x0, waiting for transfers between devices: 84.2 us -> none  [per_device(): loss_total, grad_total = lax.psum((loss_part, grad_part), ('dp', 'inner'))]
    pallas_call x0 -> x1, Pallas kernels: none -> 83.1 us  [per_device(): pl.pallas_call(kernel, out_shape=(jax.ShapeDtypeStruct((D, PROJ), F32), j...]
    psum x1 -> x0, blocking collectives: 72.8 us -> none  [per_device(): loss_total, grad_total = lax.psum((loss_part, grad_part), ('dp', 'inner'))]
    dot_general x19 -> x0, matrix products: 63.5 us -> none  [the longest x8 23.9 us: add_rows(): return total + jnp.dot(probs, columns, preferred_element_type=jnp.float32)]
    all_gather x1 -> x0, waiting for transfers between devices: 58.9 us -> none  [per_device(): full = lax.all_gather(group, 'dp', axis=0, tiled=True)]
    all_gather x1 -> x0, blocking collectives: 34.8 us -> none  [per_device(): group = lax.all_gather(ub, 'inner', axis=0, tiled=True)]
    unnamed x7 -> x1, local copies, waits for them, and re-layouts: 17 us -> 3.04 us
  transfers between devices with their start and end apart: 3 -> 0, of which waited for: 3 -> 0; matrix products, arithmetic and copies ran while one was open for 3% -> 0% of each run, Pallas kernels for 0% -> 0%
where the time goes in v1:
time: 89.5 us; the launch traced here: 89.2 us
  Pallas kernels  83.1 us (93%)
  local copies, waits for them, and re-layouts  4.24 us (5%)
  other arithmetic  1.29 us (1%)
    pallas_call x1, Pallas kernels, per_device(): pl.pallas_call(kernel, out_shape=(jax.ShapeDtypeStruct((D, PROJ), F32), j...  83.1 us
    unnamed x1, local copies, waits for them, and re-layouts  3.04 us

profile of v1, /device:TPU:1, one launch (start us, length us, event | category | flops | bytes accessed | tf_op | source)
XLA Modules:
  0.0 89.2 jit_solution(7887272517352851032)
XLA Ops:
  0.6 0.7 fusion.6
  1.3 0.6 fusion.2.code_ref
  1.9 83.1 %simclr_head.1 = (f32[4096,128]{1,0:T(8,128)}, f32[8,128]{1,0:T(8,128)}) custom-call(bf16[256,4096]{1,0:T(8,128)(2,1)} %f_hbm.1, bf16[4096,128]{1,0:T(8,128)(2,1)} %w_hbm.1, bf16[16,128]{1,0:T(8,128)(2,1)} %fusion.2.code_ref), custom_call_target="tpu_custom_call" | custom-call | tf_op jit(solution)/shard_map/simclr_head/pallas_call | solution.py:455
  85.0 1.2 %slice.3 = f32[1,1]{1,0:T(1,128)} slice(f32[8,128]{1,0:T(8,128)} %get-tuple-element.4), slice={[0:1], [0:1]} | slice | bytes 8 | tf_op jit(solution)/shard_map/slice | solution.py:520
  86.2 3.0 %copy.6 = f32[4096,128]{1,0:T(8,128)} copy(f32[4096,128]{1,0:T(8,128)} %get-tuple-element.11) | data formatting | bytes 4194304

commit v2 on v1

--- a/solution.py
+++ b/solution.py
@@ -11,14 +11,15 @@
 VIEWS = 32768
 D = 4096
 HALF = D // 2
+QUARTER = D // 4
 PROJ = 128
 OWN = 256
+GROUP = 4 * OWN
 SLOT = OWN + 16
 INV_TAU = 5.0
 SCALE2 = INV_TAU * 1.4426950408889634
 NT = (((1,), (1,)), ((), ()))
 TN = (((0,), (0,)), ((), ()))
-EXACT = lax.Precision.HIGHEST
 
 ROW_OFFS = [(dx, dc) for dc in range(2) for dx in range(4)]
 ROW_OF = {off: slot for slot, off in enumerate(ROW_OFFS)}
@@ -27,6 +28,7 @@
     key=lambda o: (min(o[0], 4 - o[0]) + min(o[1], 4 - o[1]), o),
 )
 COL_OF = {off: slot for slot, off in enumerate(COL_OFFS)}
+RING_AXIS = {slot: int(off[0] == 0) for slot, off in enumerate(COL_OFFS) if slot and 0 in off}
 PARTS = ("x", "y", "z", "m")
 PART_ROWS = HALF // len(PARTS)
 RING_ROWS = PART_ROWS // 4
@@ -113,33 +115,70 @@
 
 
 def kernel(
-    f_hbm, w_hbm, code_ref, g_hbm, loss_ref,
+    f_hbm, w_hbm, partner_ref, g_ref, loss_ref,
     feat, weight, feat_sib, u_ref, norm_ref, rows, cols, expo, acc,
     sums, sums_in, wts, wts_in, wide, paired, uw, quad, quad_sib, quad_ring,
     dz_own, dz_sib, grad, g1_in, g1, g2_in, out, loss1, loss2,
     load_sem, x_send, col_recv, row_recv, feat_recv, sum_recv, wt_recv, loss_recv1, loss_recv2,
     qs_recv, qr_recv, dz_recv, g1_recv, g2_recv, ag_recv, ring_recv, rel_recv, store_sem,
 ):
+    sent = [
+        (rows.at[pl.ds(0, 7 * SLOT)], 0),
+        (cols.at[pl.ds(0, 15 * OWN)], 1),
+        (feat_sib, 2),
+        (sums_in.at[pl.ds(0, 7)], 3),
+        (wts_in.at[pl.ds(0, 15)], 4),
+        (loss1.at[pl.ds(0, 7)], 5),
+        (quad_sib, 6),
+        (quad_ring.at[pl.ds(0, 3)], 7),
+        (loss2.at[pl.ds(0, 15)], 8),
+        (dz_sib, 9),
+        (grad.at[pl.ds(0, 12 * RING_ROWS)], 10),
+        (grad.at[pl.ds(0, 60 * TILE)], 11),
+        (grad.at[pl.ds(0, 60 * TILE)], 12),
+        (grad.at[pl.ds(0, 12 * RING_ROWS)], 13),
+        (grad, 14),
+    ]
     x, y, z, c = coords()
+    loads = []
+    for k in range(4):
+        depth = pl.ds(k * QUARTER, QUARTER)
+        loads.append(
+            (
+                pltpu.make_async_copy(w_hbm.at[depth], weight.at[depth], load_sem.at[k]),
+                pltpu.make_async_copy(f_hbm.at[:, depth], feat.at[:, depth], load_sem.at[4 + k]),
+            )
+        )
+    for pair in loads:
+        for load in pair:
+            load.start()
     barrier = pltpu.get_barrier_semaphore()
     peers = all_peers()
     for off in peers:
         pl.semaphore_signal(barrier, inc=1, device_id=peer(*off), device_id_type=MESH)
-    load_w = pltpu.make_async_copy(w_hbm, weight, load_sem.at[0])
-    load_f = pltpu.make_async_copy(f_hbm, feat, load_sem.at[1])
-    load_w.start()
-    load_f.start()
-    load_w.wait()
-    load_f.wait()
-
-    zed = jnp.dot(feat[...], weight[...], preferred_element_type=F32)
+
+    owner_of, place_of = partner_ref[...] // OWN, partner_ref[...] % OWN
+    at = lax.broadcasted_iota(jnp.int32, (16, PROJ), 0)
+    code = jnp.zeros((16, PROJ), F32)
+    for k, row in enumerate((owner_of[0:1], owner_of[1:2], place_of[0:1], place_of[1:2])):
+        code = jnp.where(at == k, row.astype(F32), code)
+    rows[OWN:SLOT, :] = code.astype(BF16)
+
+    zed = None
+    for k, pair in enumerate(loads):
+        for load in pair:
+            load.wait()
+        term = jnp.dot(
+            feat[:, k * QUARTER : (k + 1) * QUARTER], weight[k * QUARTER : (k + 1) * QUARTER, :],
+            preferred_element_type=F32,
+        )
+        zed = term if zed is None else zed + term
     norm = jnp.sqrt(jnp.sum(zed * zed, axis=1, keepdims=True) + 1e-06)
     u = zed / norm
     u_ref[...] = u
     norm_ref[...] = jnp.broadcast_to(norm, (OWN, PROJ))
     ub = u.astype(BF16)
     rows[0:OWN, :] = ub
-    rows[OWN:SLOT, :] = code_ref[...]
     cols[0:OWN, :] = ub
     pl.semaphore_wait(barrier, len(peers))
 
@@ -149,14 +188,44 @@
     def col_slot(slot):
         return cols.at[pl.ds(slot * OWN, OWN)]
 
-    for dx in (2, 1, 3):
+    def col_half(slot, half):
+        return cols.at[pl.ds(slot * OWN + half * (OWN // 2), OWN // 2)]
+
+    for dx in (1, 3, 2):
         to = ROW_OF[neg_row((dx, 0))]
         send(row_slot(0), row_slot(to), x_send.at[0], row_recv.at[to], peer(dx=dx))
     send(row_slot(0), row_slot(4), x_send.at[0], row_recv.at[4], peer(dc=1))
-    for slot in range(1, 16):
-        dy, dz = COL_OFFS[slot]
-        to = COL_OF[neg_col((dy, dz))]
-        send(col_slot(0), col_slot(to), x_send.at[1], col_recv.at[to], peer(dy=dy, dz=dz))
+    for turn in range(2):
+        for d in (1, 3, 2):
+            for axis in range(2):
+                half = axis ^ turn
+                off = (d, 0) if axis == 0 else (0, d)
+                to = COL_OF[neg_col(off)]
+                send(
+                    col_half(0, half), col_half(to, half), x_send.at[1],
+                    col_recv.at[to, half], peer(dy=off[0], dz=off[1]),
+                )
+
+    def pass_on(axis, d):
+        off = (d, 0) if axis == 0 else (0, d)
+        slot = COL_OF[off]
+        wait_bytes(col_half(slot, axis), col_recv.at[slot, axis])
+        for e in (1, 3, 2):
+            hop = (0, e) if axis == 0 else (e, 0)
+            to = COL_OF[((off[0] - hop[0]) % 4, (off[1] - hop[1]) % 4)]
+            send(
+                col_half(slot, axis), col_half(to, axis), x_send.at[1],
+                col_recv.at[to, axis], peer(dy=hop[0], dz=hop[1]),
+            )
+
+    def pass_row(slot):
+        wait_bytes(row_slot(slot), row_recv.at[slot])
+        send(row_slot(slot), row_slot(4 + slot), x_send.at[0], row_recv.at[4 + slot], peer(dc=1))
+
+    for d in (1, 3, 2):
+        pass_on(0, d)
+        pass_on(1, d)
+        pass_row(d)
     send(
         feat.at[:, pl.ds(pl.multiple_of((1 - c) * HALF, HALF), HALF)], feat_sib,
         x_send.at[2], feat_recv.at[0], peer(dc=1),
@@ -171,43 +240,54 @@
     def scores(slot, first):
         return jnp.exp2(
             lax.dot_general(
-                rows[slot * SLOT : slot * SLOT + OWN, :], cols[pl.ds(first, OWN), :], NT,
+                rows[slot * SLOT : slot * SLOT + OWN, :], cols[pl.ds(first, GROUP), :], NT,
                 preferred_element_type=F32,
             )
             * SCALE2
         )
 
+    for slot in range(1, 4):
+        wait_bytes(col_half(slot, 1 - RING_AXIS[slot]), col_recv.at[slot, 1 - RING_AXIS[slot]])
     for slot in (0, 4, 1, 3, 2, 5, 7, 6):
-        if slot:
+        if slot > 3:
             wait_bytes(row_slot(slot), row_recv.at[slot])
-        if slot in (1, 2, 3):
-            send(row_slot(slot), row_slot(4 + slot), x_send.at[0], row_recv.at[4 + slot], peer(dc=1))
         e = scores(slot, 0)
         if slot == 0:
-            at_row = lax.broadcasted_iota(jnp.int32, (OWN, OWN), 0)
-            at_col = lax.broadcasted_iota(jnp.int32, (OWN, OWN), 1)
+            at_row = lax.broadcasted_iota(jnp.int32, (OWN, GROUP), 0)
+            at_col = lax.broadcasted_iota(jnp.int32, (OWN, GROUP), 1)
             e = jnp.where(at_row == at_col, 0.0, e)
-        expo[slot * OWN : (slot + 1) * OWN, 0:OWN] = e.astype(BF16)
+        expo[slot * OWN : (slot + 1) * OWN, 0:GROUP] = e.astype(BF16)
         acc[slot * OWN : (slot + 1) * OWN, :] = lanes(e)
 
-    def pass1(step, carry):
-        first = pl.multiple_of(step * OWN, OWN)
-        wait_bytes(cols.at[pl.ds(first, OWN)], col_recv.at[step])
+    for group in range(1, 4):
+        for slot in range(4 * group, 4 * group + 4):
+            for half in range(2):
+                if slot not in RING_AXIS or half != RING_AXIS[slot]:
+                    wait_bytes(col_half(slot, half), col_recv.at[slot, half])
         for slot in range(8):
-            e = scores(slot, first)
-            expo[slot * OWN : (slot + 1) * OWN, pl.ds(first, OWN)] = e.astype(BF16)
+            e = scores(slot, group * GROUP)
+            expo[slot * OWN : (slot + 1) * OWN, group * GROUP : (group + 1) * GROUP] = e.astype(BF16)
             acc[slot * OWN : (slot + 1) * OWN, :] += lanes(e)
-        return carry
-
-    lax.fori_loop(1, 16, pass1, 0)
-
-    ones = jnp.ones((8, PROJ), F32)
+
+    eye = lax.broadcasted_iota(jnp.int32, (PROJ, PROJ), 0) == lax.broadcasted_iota(
+        jnp.int32, (PROJ, PROJ), 1
+    )
+
+    def to_row(column):
+        return jnp.sum(jnp.where(eye, column, 0.0), axis=0, keepdims=True)
+
+    def to_column(row):
+        halves = [
+            jnp.sum(jnp.where(eye, row[:, h * PROJ : (h + 1) * PROJ], 0.0), axis=1, keepdims=True)
+            for h in range(2)
+        ]
+        return jnp.broadcast_to(jnp.concatenate(halves, axis=0), (OWN, PROJ))
+
     for slot in range(8):
-        part = lax.dot_general(
-            ones, acc[slot * OWN : (slot + 1) * OWN, :], NT,
-            preferred_element_type=F32, precision=EXACT,
-        )
-        sums[slot : slot + 1, :] = part[0:1, :]
+        for h in range(2):
+            first = slot * OWN + h * PROJ
+            column = jnp.sum(acc[first : first + PROJ, :], axis=1, keepdims=True)
+            sums[slot : slot + 1, h * PROJ : (h + 1) * PROJ] = to_row(column)
     for slot in (2, 6, 1, 3, 5, 7, 4):
         dx, dc = ROW_OFFS[slot]
         to = ROW_OF[neg_row((dx, dc))]
@@ -215,22 +295,12 @@
 
     for slot in range(16):
         wide[:, slot * PROJ : (slot + 1) * PROJ] = cols[slot * OWN : (slot + 1) * OWN, :]
-    sel_row = lax.broadcasted_iota(jnp.int32, (16, PROJ), 0)
     lane = lax.broadcasted_iota(jnp.int32, (OWN, PROJ), 1).astype(F32)
 
-    def column_of(code, at):
-        halves = [
-            lax.dot_general(
-                code, jnp.where(sel_row == at + h, 1.0, 0.0).astype(BF16), TN,
-                preferred_element_type=F32,
-            )
-            for h in range(2)
-        ]
-        return jnp.concatenate(halves, axis=0)
-
     def partners(slot, pos):
-        code = rows[slot * SLOT + OWN : (slot + 1) * SLOT, :]
-        owner, place = column_of(code, 0), column_of(code, 2)
+        code = rows[slot * SLOT + OWN : (slot + 1) * SLOT, :].astype(F32)
+        owner = to_column(jnp.concatenate([code[0:1], code[1:2]], axis=1))
+        place = to_column(jnp.concatenate([code[2:3], code[3:4]], axis=1))
         hot = jnp.concatenate(
             [jnp.where(place == lane, 1.0, 0.0), jnp.where(place == lane + PROJ, 1.0, 0.0)], axis=1
         ).astype(BF16)
@@ -276,25 +346,23 @@
         to = ROW_OF[neg_row((dx, dc))]
         send(loss1.at[me1], loss1.at[me1], x_send.at[5], loss_recv1.at[to], peer(dx=dx, dc=dc))
 
-    sel8 = jnp.where(lax.broadcasted_iota(jnp.int32, (8, PROJ), 0) == 0, 1.0, 0.0)
-
-    def weigh(slot, table):
-        w = lax.dot_general(table, sel8, TN, preferred_element_type=F32, precision=EXACT)
+    def weigh(slot, row):
         block = cols[slot * OWN : (slot + 1) * OWN, :]
         uw[slot * OWN : (slot + 1) * OWN, 0:PROJ] = block
-        uw[slot * OWN : (slot + 1) * OWN, PROJ : 2 * PROJ] = (block.astype(F32) * w).astype(BF16)
-
-    weigh(0, wts[...])
+        uw[slot * OWN : (slot + 1) * OWN, PROJ : 2 * PROJ] = (
+            block.astype(F32) * to_column(row)
+        ).astype(BF16)
+
+    weigh(0, wts[0:1, :])
     for slot in range(1, 16):
         wait_bytes(wts_in.at[slot], wt_recv.at[slot])
-        weigh(slot, wts_in[slot])
+        weigh(slot, wts_in[slot, 0:1, :])
 
     def terms(slot):
         both = jnp.dot(
             expo[slot * OWN : (slot + 1) * OWN, :], uw[...], preferred_element_type=F32
         )
-        sel = jnp.where(lax.broadcasted_iota(jnp.int32, (8, PROJ), 0) == slot, 1.0, 0.0)
-        w = lax.dot_general(wts[...], sel, TN, preferred_element_type=F32, precision=EXACT)
+        w = to_column(wts[slot : slot + 1, :])
         return (
             w * both[:, 0:PROJ] + both[:, PROJ : 2 * PROJ]
             - 2.0 * paired[slot * OWN : (slot + 1) * OWN, :]
@@ -303,11 +371,15 @@
     def quad_slot(slot):
         return quad.at[pl.ds(slot * OWN, OWN)]
 
-    for slot in (6, 5, 7, 4):
-        quad[slot * OWN : (slot + 1) * OWN, :] = terms(slot)
-        send(quad_slot(slot), quad_sib.at[slot - 4], x_send.at[6], qs_recv.at[slot - 4], peer(dc=1))
-    for slot in (2, 1, 3, 0):
+    for slot in (6, 5, 2, 7, 1, 4, 3, 0):
         part = terms(slot)
+        if slot > 3:
+            quad[slot * OWN : (slot + 1) * OWN, :] = part
+            send(
+                quad_slot(slot), quad_sib.at[slot - 4], x_send.at[6], qs_recv.at[slot - 4],
+                peer(dc=1),
+            )
+            continue
         wait_bytes(quad_sib.at[slot], qs_recv.at[slot])
         quad[slot * OWN : (slot + 1) * OWN, :] = part + quad_sib[slot]
         if slot:
@@ -409,7 +481,7 @@
             send(block, block, x_send.at[14], rel_recv.at[p, d], peer(dc=1))
     half = out.at[pl.ds(pl.multiple_of(base, HALF), HALF)]
     store1 = pltpu.make_async_copy(
-        half, g_hbm.at[pl.ds(pl.multiple_of(base, HALF), HALF)], store_sem.at[0]
+        half, g_ref.at[pl.ds(pl.multiple_of(base, HALF), HALF)], store_sem.at[0]
     )
     store1.start()
 
@@ -418,45 +490,30 @@
     total = loss2[0]
     for k in range(1, 16):
         total = total + loss2[k]
-    loss_ref[...] = total * (1.0 / VIEWS)
+    loss_ref[...] = total[0:1, 0:1] * (1.0 / VIEWS)
 
     for d in (0, 1, 3, 2):
         for p in range(len(PARTS)):
             wait_bytes(out.at[pl.ds(0, RING_ROWS)], rel_recv.at[p, d])
     other = pl.multiple_of((1 - c) * HALF, HALF)
     store2 = pltpu.make_async_copy(
-        out.at[pl.ds(other, HALF)], g_hbm.at[pl.ds(other, HALF)], store_sem.at[1]
+        out.at[pl.ds(other, HALF)], g_ref.at[pl.ds(other, HALF)], store_sem.at[1]
     )
     store2.start()
 
-    wait_bytes(rows.at[pl.ds(0, 7 * SLOT)], x_send.at[0])
-    wait_bytes(cols.at[pl.ds(0, 15 * OWN)], x_send.at[1])
-    wait_bytes(feat_sib, x_send.at[2])
-    wait_bytes(sums_in.at[pl.ds(0, 7)], x_send.at[3])
-    wait_bytes(wts_in.at[pl.ds(0, 15)], x_send.at[4])
-    wait_bytes(loss1.at[pl.ds(0, 7)], x_send.at[5])
-    wait_bytes(quad_sib, x_send.at[6])
-    wait_bytes(quad_ring.at[pl.ds(0, 3)], x_send.at[7])
-    wait_bytes(loss2.at[pl.ds(0, 15)], x_send.at[8])
-    wait_bytes(dz_sib, x_send.at[9])
-    wait_bytes(grad.at[pl.ds(0, 12 * RING_ROWS)], x_send.at[10])
-    wait_bytes(grad.at[pl.ds(0, 60 * TILE)], x_send.at[11])
-    wait_bytes(grad.at[pl.ds(0, 60 * TILE)], x_send.at[12])
-    wait_bytes(grad.at[pl.ds(0, 12 * RING_ROWS)], x_send.at[13])
-    wait_bytes(grad, x_send.at[14])
+    for ref, at in sent:
+        wait_bytes(ref, x_send.at[at])
     store1.wait()
     store2.wait()
 
 
 def per_device(features, proj_weight, partner):
-    code = jnp.concatenate([partner // OWN, partner % OWN]).reshape(4, PROJ)
-    code = jnp.pad(code, ((0, 12), (0, 0))).astype(BF16)
     dma = pltpu.SemaphoreType.DMA
     grad, loss = pl.pallas_call(
         kernel,
         out_shape=(
             jax.ShapeDtypeStruct((D, PROJ), F32),
-            jax.ShapeDtypeStruct((8, PROJ), F32),
+            jax.ShapeDtypeStruct((1, 1), F32),
         ),
         in_specs=[
             pl.BlockSpec(memory_space=pl.ANY),
@@ -493,9 +550,9 @@
             pltpu.VMEM((D, PROJ), F32),
             pltpu.VMEM((8, 8, PROJ), F32),
             pltpu.VMEM((16, 8, PROJ), F32),
-            dma((2,)),
+            dma((8,)),
             dma((15,)),
-            dma((16,)),
+            dma((16, 2)),
             dma((8,)),
             dma((1,)),
             dma((8,)),
@@ -516,8 +573,8 @@
             collective_id=0, has_side_effects=True, vmem_limit_bytes=56 * 2**20
         ),
         name="simclr_head",
-    )(features, proj_weight, code)
-    return loss[0, 0], grad
+    )(features, proj_weight, partner.reshape(2, PROJ))
+    return loss.reshape(()), grad
 
 
 def solution(mesh):

time: 89.5 us -> 77.9 us (0.87)
  Pallas kernels: 83.1 us -> 72.3 us
  between operations: 0.64 us -> 2.37 us
  other arithmetic: 1.29 us -> 0 us
  local copies, waits for them, and re-layouts: 4.24 us -> 3.05 us
    pallas_call x1, Pallas kernels: 83.1 us -> 72.3 us  [per_device(): pl.pallas_call(kernel, out_shape=(jax.ShapeDtypeStruct((D, PROJ), F32), j...]
    concatenate x2 -> x0, other arithmetic: 1.29 us -> none  [per_device(): code = jnp.concatenate([partner // OWN, partner % OWN]).reshape(4, PROJ)]
    slice x1 -> x0, local copies, waits for them, and re-layouts: 1.19 us -> none  [per_device(): return (loss[0, 0], grad)]
where the time goes in v2:
time: 77.9 us; the launch traced here: 77.7 us
  Pallas kernels  72.3 us (93%)
  local copies, waits for them, and re-layouts  3.05 us (4%)
  between operations  2.37 us (3%)
    pallas_call x1, Pallas kernels, per_device(): pl.pallas_call(kernel, out_shape=(jax.ShapeDtypeStruct((D, PROJ), F32), j...  72.3 us
    unnamed x1, local copies, waits for them, and re-layouts  3.05 us

profile of v2, /device:TPU:1, one launch (start us, length us, event | category | flops | bytes accessed | tf_op | source)
XLA Modules:
  0.0 77.7 jit_solution(16783454448980476741)
XLA Ops:
  0.6 72.3 %simclr_head.1 = (f32[4096,128]{1,0:T(8,128)}, f32[1,1]{1,0:T(1,128)}) custom-call(bf16[256,4096]{1,0:T(8,128)(2,1)} %f_hbm.1, bf16[4096,128]{1,0:T(8,128)(2,1)} %w_hbm.1, s32[2,128]{1,0:T(2,128)} %bitcast.2), custom_call_target="tpu_custom_call" | custom-call | tf_op jit(solution)/shard_map/simclr_head/pallas_call | solution.py:512
  73.6 3.0 %copy.8 = f32[4096,128]{1,0:T(8,128)} copy(f32[4096,128]{1,0:T(8,128)} %get-tuple-element.9) | data formatting | bytes 4194304

commit v3 on v2

--- a/solution.py
+++ b/solution.py
@@ -29,10 +29,8 @@
 )
 COL_OF = {off: slot for slot, off in enumerate(COL_OFFS)}
 RING_AXIS = {slot: int(off[0] == 0) for slot, off in enumerate(COL_OFFS) if slot and 0 in off}
-PARTS = ("x", "y", "z", "m")
-PART_ROWS = HALF // len(PARTS)
-RING_ROWS = PART_ROWS // 4
-TILE = RING_ROWS // 16
+TILES = (16, 8, 8)
+STARTS = (0, 1024, 1536)
 
 
 def neg_col(off):
@@ -53,53 +51,56 @@
     return ((x % 2) * 8 + y * 2 + c, z * 2 + x // 2)
 
 
-def peer(dx=0, dy=0, dz=0, dc=0):
-    x, y, z, c = coords()
-    return device_at((x + dx) % 4, (y + dy) % 4, (z + dz) % 4, (c + dc) % 2)
-
-
-def ring_peer(part, d):
-    c = coords()[3]
-    if part == "x":
-        return peer(dx=d)
-    if part == "y":
-        return peer(dy=d)
-    if part == "z":
-        return peer(dz=d)
-    return peer(dx=d * (1 - c), dy=d * c)
-
-
-def plane_peer(part, d1, d2):
-    c = coords()[3]
-    if part == "x":
-        return peer(dy=d1, dz=d2)
-    if part == "y":
-        return peer(dx=d1, dz=d2)
-    if part == "z":
-        return peer(dx=d1, dy=d2)
-    return peer(dx=d1 * c, dy=d1 * (1 - c), dz=d2)
-
-
-def part_place(part):
-    x, y, z, c = coords()
-    if part == "x":
-        return x, y, z
-    if part == "y":
-        return y, x, z
-    if part == "z":
-        return z, x, y
-    return x * (1 - c) + y * c, y * (1 - c) + x * c, z
-
-
-def all_peers():
-    offs = []
-    for dx in range(4):
-        for dy in range(4):
-            for dz in range(4):
-                if (dx, dy, dz) != (0, 0, 0) and 0 in (dx, dy, dz):
-                    offs.append((dx, dy, dz, 0))
-    offs += [(dx, 0, 0, 1) for dx in range(4)]
-    return offs
+class Torus:
+    def __init__(self):
+        x, y, z, c = coords()
+        self.xs, self.ys, self.zs = ([(v + d) % 4 for d in range(4)] for v in (x, y, z))
+        self.cs = [c, 1 - c]
+        self.x_dp = [v % 2 * 8 for v in self.xs]
+        self.x_inner = [v // 2 for v in self.xs]
+        self.y_dp = [v * 2 for v in self.ys]
+        self.z_inner = [v * 2 for v in self.zs]
+
+    def peer(self, dx=0, dy=0, dz=0, dc=0):
+        return (
+            self.x_dp[dx] + self.y_dp[dy] + self.cs[dc],
+            self.z_inner[dz] + self.x_inner[dx],
+        )
+
+    def pick(self, a, b):
+        return a * self.cs[1] + b * self.cs[0]
+
+    def pick_peer(self, a, b):
+        return self.pick(a[0], b[0]), self.pick(a[1], b[1])
+
+    def ring_at(self, part, d):
+        if part == 2:
+            return self.zs[d]
+        ends = (self.xs[d], self.ys[d])
+        return self.pick(*(ends if part == 0 else ends[::-1]))
+
+    def plane_at(self, part, d1, d2):
+        if part == 2:
+            return self.xs[d1] * 4 + self.ys[d2]
+        ends = (self.ys[d1], self.xs[d1])
+        return self.pick(*(ends if part == 0 else ends[::-1])) * 4 + self.zs[d2]
+
+    def ring_peer(self, part, d):
+        if part == 2:
+            return self.peer(dz=d)
+        ends = (self.peer(dx=d), self.peer(dy=d))
+        return self.pick_peer(*(ends if part == 0 else ends[::-1]))
+
+    def plane_peer(self, part, d1, d2):
+        if part == 2:
+            return self.peer(dx=d1, dy=d2)
+        ends = (self.peer(dy=d1, dz=d2), self.peer(dx=d1, dz=d2))
+        return self.pick_peer(*(ends if part == 0 else ends[::-1]))
+
+
+def ring_peers():
+    offs = [off for d in (1, 3, 2) for off in ((d, 0, 0, 0), (0, d, 0, 0), (0, 0, d, 0))]
+    return offs + [(0, 0, 0, 1)]
 
 
 def send(src, dst, send_sem, recv_sem, device):
@@ -118,7 +119,8 @@
     f_hbm, w_hbm, partner_ref, g_ref, loss_ref,
     feat, weight, feat_sib, u_ref, norm_ref, rows, cols, expo, acc,
     sums, sums_in, wts, wts_in, wide, paired, uw, quad, quad_sib, quad_ring,
-    dz_own, dz_sib, grad, g1_in, g1, g2_in, out, loss1, loss2,
+    dz_own, dz_sib, grad, g1_in_a, g1_in_b, g1_in_c, g1_a, g1_b, g1_c,
+    g2_in_a, g2_in_b, g2_in_c, out, loss1, loss2,
     load_sem, x_send, col_recv, row_recv, feat_recv, sum_recv, wt_recv, loss_recv1, loss_recv2,
     qs_recv, qr_recv, dz_recv, g1_recv, g2_recv, ag_recv, ring_recv, rel_recv, store_sem,
 ):
@@ -133,13 +135,15 @@
         (quad_ring.at[pl.ds(0, 3)], 7),
         (loss2.at[pl.ds(0, 15)], 8),
         (dz_sib, 9),
-        (grad.at[pl.ds(0, 12 * RING_ROWS)], 10),
-        (grad.at[pl.ds(0, 60 * TILE)], 11),
-        (grad.at[pl.ds(0, 60 * TILE)], 12),
-        (grad.at[pl.ds(0, 12 * RING_ROWS)], 13),
+        (grad.at[pl.ds(0, 3 * HALF // 4)], 10),
+        (grad.at[pl.ds(0, 15 * sum(TILES))], 11),
+        (grad.at[pl.ds(0, 15 * sum(TILES))], 12),
+        (grad.at[pl.ds(0, 3 * HALF // 4)], 13),
         (grad, 14),
     ]
-    x, y, z, c = coords()
+    torus = Torus()
+    peer = torus.peer
+    x, y, z, c = torus.xs[0], torus.ys[0], torus.zs[0], torus.cs[0]
     loads = []
     for k in range(4):
         depth = pl.ds(k * QUARTER, QUARTER)
@@ -153,7 +157,7 @@
         for load in pair:
             load.start()
     barrier = pltpu.get_barrier_semaphore()
-    peers = all_peers()
+    peers = ring_peers()
     for off in peers:
         pl.semaphore_signal(barrier, inc=1, device_id=peer(*off), device_id_type=MESH)
 
@@ -386,6 +390,41 @@
             to = (-slot) % 4
             send(quad_slot(slot), quad_ring.at[to], x_send.at[7], qr_recv.at[to], peer(dx=slot))
 
+    summed = quad[0:OWN, :]
+    for d in (1, 3, 2):
+        wait_bytes(quad_ring.at[d], qr_recv.at[d])
+        summed = summed + quad_ring[d]
+    du = INV_TAU * summed
+    uu = u_ref[...]
+    dz_own[...] = (
+        (du - uu * jnp.sum(uu * du, axis=1, keepdims=True)) / norm_ref[...]
+    ).astype(BF16)
+    send(dz_own, dz_sib, x_send.at[9], dz_recv.at[0], peer(dc=1))
+
+    mine = pl.multiple_of(c * HALF, HALF)
+    grad[...] = lax.dot_general(
+        feat[:, pl.ds(mine, HALF)], dz_own[...], TN, preferred_element_type=F32
+    )
+    wait_bytes(feat_sib, feat_recv.at[0])
+    wait_bytes(dz_sib, dz_recv.at[0])
+    grad[...] += lax.dot_general(feat_sib[...], dz_sib[...], TN, preferred_element_type=F32)
+
+    g1_in, g1, g2_in = (g1_in_a, g1_in_b, g1_in_c), (g1_a, g1_b, g1_c), (g2_in_a, g2_in_b, g2_in_c)
+    parts = (2, 1, 0)
+
+    def ring_block(part, d, base=0):
+        span = 16 * TILES[part]
+        first = base + STARTS[part] + torus.ring_at(part, d) * span
+        return pl.ds(pl.multiple_of(first, span), span)
+
+    for d in (2, 1, 3):
+        for part in parts:
+            at = (-d) % 4
+            send(
+                grad.at[ring_block(part, d)], g1_in[part].at[at],
+                x_send.at[10], g1_recv.at[part, at], torus.ring_peer(part, d),
+            )
+
     for slot in range(1, 8):
         wait_bytes(loss1.at[0], loss_recv1.at[slot])
     total = loss1[0]
@@ -398,92 +437,59 @@
         to = COL_OF[neg_col((dy, dz))]
         send(loss2.at[me2], loss2.at[me2], x_send.at[8], loss_recv2.at[to], peer(dy=dy, dz=dz))
 
-    summed = quad[0:OWN, :]
-    for d in (1, 3, 2):
-        wait_bytes(quad_ring.at[d], qr_recv.at[d])
-        summed = summed + quad_ring[d]
-    du = INV_TAU * summed
-    uu = u_ref[...]
-    dz_own[...] = (
-        (du - uu * jnp.sum(uu * du, axis=1, keepdims=True)) / norm_ref[...]
-    ).astype(BF16)
-    send(dz_own, dz_sib, x_send.at[9], dz_recv.at[0], peer(dc=1))
-
-    mine = pl.multiple_of(c * HALF, HALF)
-    grad[...] = lax.dot_general(
-        feat[:, pl.ds(mine, HALF)], dz_own[...], TN, preferred_element_type=F32
-    )
-    wait_bytes(feat_sib, feat_recv.at[0])
-    wait_bytes(dz_sib, dz_recv.at[0])
-    grad[...] += lax.dot_general(feat_sib[...], dz_sib[...], TN, preferred_element_type=F32)
-
-    def ring_block(part, t):
-        return pl.ds(pl.multiple_of(part * PART_ROWS + t * RING_ROWS, RING_ROWS), RING_ROWS)
-
-    places = [part_place(name) for name in PARTS]
-    for d in (2, 1, 3):
-        for p, name in enumerate(PARTS):
-            t = places[p][0]
-            at = (-d) % 4
-            send(
-                grad.at[ring_block(p, (t + d) % 4)], g1_in.at[p, at],
-                x_send.at[10], g1_recv.at[p, at], ring_peer(name, d),
-            )
-    for p, name in enumerate(PARTS):
-        t, s1, s2 = places[p]
-        total = grad[ring_block(p, t), :]
-        for d in range(1, 4):
-            wait_bytes(g1_in.at[p, d], g1_recv.at[p, d])
-            total = total + g1_in[p, d]
-        g1[p] = total
+    for part in parts:
+        total = grad[ring_block(part, 0), :]
+        for d in (1, 3, 2):
+            wait_bytes(g1_in[part].at[d], g1_recv.at[part, d])
+            total = total + g1_in[part][d]
+        g1[part][...] = total
+        tile = TILES[part]
         for slot in range(15, 0, -1):
             d1, d2 = COL_OFFS[slot]
             to = COL_OF[neg_col((d1, d2))]
-            at = ((s1 + d1) % 4) * 4 + (s2 + d2) % 4
+            at = pl.multiple_of(torus.plane_at(part, d1, d2) * tile, tile)
             send(
-                g1.at[p, pl.ds(pl.multiple_of(at * TILE, TILE), TILE)],
-                g2_in.at[p, pl.ds(to * TILE, TILE)],
-                x_send.at[11], g2_recv.at[p], plane_peer(name, d1, d2),
+                g1[part].at[pl.ds(at, tile)], g2_in[part].at[pl.ds(to * tile, tile)],
+                x_send.at[11], g2_recv.at[part], torus.plane_peer(part, d1, d2),
             )
     base = c * HALF
-    for p, name in enumerate(PARTS):
-        t, s1, s2 = places[p]
-        total = g1[p, pl.ds(pl.multiple_of((s1 * 4 + s2) * TILE, TILE), TILE), :]
-        wait_bytes(g2_in.at[p, pl.ds(TILE, 15 * TILE)], g2_recv.at[p])
+    for part in parts:
+        tile = TILES[part]
+        place = torus.plane_at(part, 0, 0) * tile
+        total = g1[part][pl.ds(pl.multiple_of(place, tile), tile), :]
+        wait_bytes(g2_in[part].at[pl.ds(tile, 15 * tile)], g2_recv.at[part])
         for slot in range(1, 16):
-            total = total + g2_in[p, slot * TILE : (slot + 1) * TILE, :]
-        at = pl.ds(
-            pl.multiple_of(base + p * PART_ROWS + t * RING_ROWS + (s1 * 4 + s2) * TILE, TILE), TILE
-        )
+            total = total + g2_in[part][slot * tile : (slot + 1) * tile, :]
+        first = base + STARTS[part] + torus.ring_at(part, 0) * 16 * tile + place
+        at = pl.ds(pl.multiple_of(first, tile), tile)
         out[at, :] = total * (1.0 / VIEWS**0.5)
         for slot in range(15, 0, -1):
             d1, d2 = COL_OFFS[slot]
-            send(out.at[at], out.at[at], x_send.at[12], ag_recv.at[p], plane_peer(name, d1, d2))
-
-    def out_block(p, t, first=base):
-        return out.at[
-            pl.ds(pl.multiple_of(first + p * PART_ROWS + t * RING_ROWS, RING_ROWS), RING_ROWS)
-        ]
-
-    for p, name in enumerate(PARTS):
-        t = places[p][0]
-        wait_bytes(out.at[pl.ds(0, 15 * TILE)], ag_recv.at[p])
-        block = out_block(p, t)
+            send(
+                out.at[at], out.at[at], x_send.at[12], ag_recv.at[part],
+                torus.plane_peer(part, d1, d2),
+            )
+
+    def store(rows_of):
+        pltpu.make_async_copy(out.at[rows_of], g_ref.at[rows_of], store_sem.at[0]).start()
+
+    for part in parts:
+        wait_bytes(out.at[pl.ds(0, 15 * TILES[part])], ag_recv.at[part])
+        block = ring_block(part, 0, base)
         for d in (2, 1, 3):
             at = (-d) % 4
-            send(block, block, x_send.at[13], ring_recv.at[p, at], ring_peer(name, d))
-        send(block, block, x_send.at[14], rel_recv.at[p, 0], peer(dc=1))
+            send(
+                out.at[block], out.at[block], x_send.at[13], ring_recv.at[part, at],
+                torus.ring_peer(part, d),
+            )
+        send(out.at[block], out.at[block], x_send.at[14], rel_recv.at[part, 0], peer(dc=1))
+        store(block)
     for d in (1, 3, 2):
-        for p, name in enumerate(PARTS):
-            t = places[p][0]
-            block = out_block(p, (t + d) % 4)
-            wait_bytes(block, ring_recv.at[p, d])
-            send(block, block, x_send.at[14], rel_recv.at[p, d], peer(dc=1))
-    half = out.at[pl.ds(pl.multiple_of(base, HALF), HALF)]
-    store1 = pltpu.make_async_copy(
-        half, g_ref.at[pl.ds(pl.multiple_of(base, HALF), HALF)], store_sem.at[0]
-    )
-    store1.start()
+        for part in parts:
+            block = ring_block(part, d, base)
+            wait_bytes(out.at[block], ring_recv.at[part, d])
+            send(out.at[block], out.at[block], x_send.at[14], rel_recv.at[part, d], peer(dc=1))
+            store(block)
 
     for slot in range(1, 16):
         wait_bytes(loss2.at[0], loss_recv2.at[slot])
@@ -492,19 +498,19 @@
         total = total + loss2[k]
     loss_ref[...] = total[0:1, 0:1] * (1.0 / VIEWS)
 
+    other = torus.cs[1] * HALF
     for d in (0, 1, 3, 2):
-        for p in range(len(PARTS)):
-            wait_bytes(out.at[pl.ds(0, RING_ROWS)], rel_recv.at[p, d])
-    other = pl.multiple_of((1 - c) * HALF, HALF)
-    store2 = pltpu.make_async_copy(
-        out.at[pl.ds(other, HALF)], g_ref.at[pl.ds(other, HALF)], store_sem.at[1]
-    )
-    store2.start()
+        for part in parts:
+            span = 16 * TILES[part]
+            ends = (torus.ys[d], torus.xs[d])
+            ring = torus.zs[d] if part == 2 else torus.pick(*(ends if part == 0 else ends[::-1]))
+            block = pl.ds(pl.multiple_of(other + STARTS[part] + ring * span, span), span)
+            wait_bytes(out.at[block], rel_recv.at[part, d])
+            store(block)
 
     for ref, at in sent:
         wait_bytes(ref, x_send.at[at])
-    store1.wait()
-    store2.wait()
+    wait_bytes(out, store_sem.at[0])
 
 
 def per_device(features, proj_weight, partner):
@@ -512,7 +518,7 @@
     grad, loss = pl.pallas_call(
         kernel,
         out_shape=(
-            jax.ShapeDtypeStruct((D, PROJ), F32),
+            pltpu.VMEM((D, PROJ), F32),
             jax.ShapeDtypeStruct((1, 1), F32),
         ),
         in_specs=[
@@ -520,7 +526,7 @@
             pl.BlockSpec(memory_space=pl.ANY),
             pl.BlockSpec(memory_space=pltpu.VMEM),
         ],
-        out_specs=(pl.BlockSpec(memory_space=pl.ANY), pl.BlockSpec(memory_space=pltpu.VMEM)),
+        out_specs=(pl.BlockSpec(memory_space=pltpu.VMEM), pl.BlockSpec(memory_space=pltpu.VMEM)),
         scratch_shapes=[
             pltpu.VMEM((OWN, D), BF16),
             pltpu.VMEM((D, PROJ), BF16),
@@ -544,9 +550,9 @@
             pltpu.VMEM((OWN, PROJ), BF16),
             pltpu.VMEM((OWN, PROJ), BF16),
             pltpu.VMEM((HALF, PROJ), F32),
-            pltpu.VMEM((4, 4, RING_ROWS, PROJ), F32),
-            pltpu.VMEM((4, RING_ROWS, PROJ), F32),
-            pltpu.VMEM((4, RING_ROWS, PROJ), F32),
+            *[pltpu.VMEM((4, 16 * tile, PROJ), F32) for tile in TILES],
+            *[pltpu.VMEM((16 * tile, PROJ), F32) for tile in TILES],
+            *[pltpu.VMEM((16 * tile, PROJ), F32) for tile in TILES],
             pltpu.VMEM((D, PROJ), F32),
             pltpu.VMEM((8, 8, PROJ), F32),
             pltpu.VMEM((16, 8, PROJ), F32),
@@ -562,12 +568,12 @@
             dma((4,)),
             dma((4,)),
             dma((1,)),
-            dma((4, 4)),
-            dma((4,)),
-            dma((4,)),
-            dma((4, 4)),
-            dma((4, 4)),
-            dma((2,)),
+            dma((3, 4)),
+            dma((3,)),
+            dma((3,)),
+            dma((3, 4)),
+            dma((3, 4)),
+            dma((1,)),
         ],
         compiler_params=pltpu.CompilerParams(
             collective_id=0, has_side_effects=True, vmem_limit_bytes=56 * 2**20

time: 77.9 us -> 75.7 us (0.972)
  local copies, waits for them, and re-layouts: 3.05 us -> 1.32 us
    unnamed x1, local copies, waits for them, and re-layouts: 3.05 us -> 1.32 us
where the time goes in v3:
time: 75.7 us; the launch traced here: 75.5 us
  Pallas kernels  71.9 us (95%)
  between operations  2.33 us (3%)
  local copies, waits for them, and re-layouts  1.32 us (2%)
    pallas_call x1, Pallas kernels, per_device(): pl.pallas_call(kernel, out_shape=(pltpu.VMEM((D, PROJ), F32), jax.ShapeDt...  71.9 us

profile of v3, /device:TPU:1, one launch (start us, length us, event | category | flops | bytes accessed | tf_op | source)
XLA Modules:
  0.0 75.5 jit_solution(4744639958758863495)
XLA Ops:
  0.6 71.9 %simclr_head.1 = (f32[4096,128]{1,0:T(8,128)S(1)}, f32[1,1]{1,0:T(1,128)}) custom-call(bf16[256,4096]{1,0:T(8,128)(2,1)} %f_hbm.1, bf16[4096,128]{1,0:T(8,128)(2,1)} %w_hbm.1, s32[2,128]{1,0:T(2,128)} %bitcast.2), custom_call_target="tpu_custom_call" | custom-call | tf_op jit(solution)/shard_map/simclr_head/pallas_call | solution.py:518
  72.5 1.3 %copy.7 = f32[4096,128]{1,0:T(8,128)} copy(f32[4096,128]{1,0:T(8,128)S(1)} %get-tuple-element.7) | data formatting | bytes 4194304

commit v4 on v3

--- a/solution.py
+++ b/solution.py
@@ -14,7 +14,7 @@
 QUARTER = D // 4
 PROJ = 128
 OWN = 256
-GROUP = 4 * OWN
+GROUPS = ((0, 4), (4, 8), (8, 12), (12, 14), (14, 16))
 SLOT = OWN + 16
 INV_TAU = 5.0
 SCALE2 = INV_TAU * 1.4426950408889634
@@ -25,7 +25,7 @@
 ROW_OF = {off: slot for slot, off in enumerate(ROW_OFFS)}
 COL_OFFS = sorted(
     [(dy, dz) for dy in range(4) for dz in range(4)],
-    key=lambda o: (min(o[0], 4 - o[0]) + min(o[1], 4 - o[1]), o),
+    key=lambda o: (0 not in o, min(o[0], 4 - o[0]) + min(o[1], 4 - o[1]), o),
 )
 COL_OF = {off: slot for slot, off in enumerate(COL_OFFS)}
 RING_AXIS = {slot: int(off[0] == 0) for slot, off in enumerate(COL_OFFS) if slot and 0 in off}
@@ -99,7 +99,7 @@
 
 
 def ring_peers():
-    offs = [off for d in (1, 3, 2) for off in ((d, 0, 0, 0), (0, d, 0, 0), (0, 0, d, 0))]
+    offs = [off for d in (2, 1, 3) for off in ((d, 0, 0, 0), (0, d, 0, 0), (0, 0, d, 0))]
     return offs + [(0, 0, 0, 1)]
 
 
@@ -116,13 +116,13 @@
 
 
 def kernel(
-    f_hbm, w_hbm, partner_ref, g_ref, loss_ref,
-    feat, weight, feat_sib, u_ref, norm_ref, rows, cols, expo, acc,
+    f_hbm, w_hbm, partner_hbm, out, loss_ref,
+    partner_ref, feat, weight, feat_sib, u_ref, norm_ref, rows, cols, expo, acc,
     sums, sums_in, wts, wts_in, wide, paired, uw, quad, quad_sib, quad_ring,
     dz_own, dz_sib, grad, g1_in_a, g1_in_b, g1_in_c, g1_a, g1_b, g1_c,
-    g2_in_a, g2_in_b, g2_in_c, out, loss1, loss2,
+    g2_in_a, g2_in_b, g2_in_c, loss1, loss2,
     load_sem, x_send, col_recv, row_recv, feat_recv, sum_recv, wt_recv, loss_recv1, loss_recv2,
-    qs_recv, qr_recv, dz_recv, g1_recv, g2_recv, ag_recv, ring_recv, rel_recv, store_sem,
+    qs_recv, qr_recv, dz_recv, g1_recv, g2_recv, ag_recv, ring_recv, rel_recv,
 ):
     sent = [
         (rows.at[pl.ds(0, 7 * SLOT)], 0),
@@ -153,6 +153,8 @@
                 pltpu.make_async_copy(f_hbm.at[:, depth], feat.at[:, depth], load_sem.at[4 + k]),
             )
         )
+    load_partner = pltpu.make_async_copy(partner_hbm, partner_ref, load_sem.at[8])
+    load_partner.start()
     for pair in loads:
         for load in pair:
             load.start()
@@ -161,6 +163,7 @@
     for off in peers:
         pl.semaphore_signal(barrier, inc=1, device_id=peer(*off), device_id_type=MESH)
 
+    load_partner.wait()
     owner_of, place_of = partner_ref[...] // OWN, partner_ref[...] % OWN
     at = lax.broadcasted_iota(jnp.int32, (16, PROJ), 0)
     code = jnp.zeros((16, PROJ), F32)
@@ -241,10 +244,10 @@
             total = total + e[:, q * PROJ : (q + 1) * PROJ]
         return total
 
-    def scores(slot, first):
+    def scores(slot, first, end):
         return jnp.exp2(
             lax.dot_general(
-                rows[slot * SLOT : slot * SLOT + OWN, :], cols[pl.ds(first, GROUP), :], NT,
+                rows[slot * SLOT : slot * SLOT + OWN, :], cols[first * OWN : end * OWN, :], NT,
                 preferred_element_type=F32,
             )
             * SCALE2
@@ -255,22 +258,22 @@
     for slot in (0, 4, 1, 3, 2, 5, 7, 6):
         if slot > 3:
             wait_bytes(row_slot(slot), row_recv.at[slot])
-        e = scores(slot, 0)
+        e = scores(slot, *GROUPS[0])
         if slot == 0:
-            at_row = lax.broadcasted_iota(jnp.int32, (OWN, GROUP), 0)
-            at_col = lax.broadcasted_iota(jnp.int32, (OWN, GROUP), 1)
+            at_row = lax.broadcasted_iota(jnp.int32, e.shape, 0)
+            at_col = lax.broadcasted_iota(jnp.int32, e.shape, 1)
             e = jnp.where(at_row == at_col, 0.0, e)
-        expo[slot * OWN : (slot + 1) * OWN, 0:GROUP] = e.astype(BF16)
+        expo[slot * OWN : (slot + 1) * OWN, 0 : GROUPS[0][1] * OWN] = e.astype(BF16)
         acc[slot * OWN : (slot + 1) * OWN, :] = lanes(e)
 
-    for group in range(1, 4):
-        for slot in range(4 * group, 4 * group + 4):
+    for first, end in GROUPS[1:]:
+        for slot in range(first, end):
             for half in range(2):
                 if slot not in RING_AXIS or half != RING_AXIS[slot]:
                     wait_bytes(col_half(slot, half), col_recv.at[slot, half])
         for slot in range(8):
-            e = scores(slot, group * GROUP)
-            expo[slot * OWN : (slot + 1) * OWN, group * GROUP : (group + 1) * GROUP] = e.astype(BF16)
+            e = scores(slot, first, end)
+            expo[slot * OWN : (slot + 1) * OWN, first * OWN : end * OWN] = e.astype(BF16)
             acc[slot * OWN : (slot + 1) * OWN, :] += lanes(e)
 
     eye = lax.broadcasted_iota(jnp.int32, (PROJ, PROJ), 0) == lax.broadcasted_iota(
@@ -362,10 +365,12 @@
         wait_bytes(wts_in.at[slot], wt_recv.at[slot])
         weigh(slot, wts_in[slot, 0:1, :])
 
-    def terms(slot):
-        both = jnp.dot(
+    def product(slot):
+        return jnp.dot(
             expo[slot * OWN : (slot + 1) * OWN, :], uw[...], preferred_element_type=F32
         )
+
+    def terms(slot, both):
         w = to_column(wts[slot : slot + 1, :])
         return (
             w * both[:, 0:PROJ] + both[:, PROJ : 2 * PROJ]
@@ -375,20 +380,25 @@
     def quad_slot(slot):
         return quad.at[pl.ds(slot * OWN, OWN)]
 
-    for slot in (6, 5, 2, 7, 1, 4, 3, 0):
-        part = terms(slot)
-        if slot > 3:
+    slot, both = None, None
+    for later in (6, 5, 7, 2, 4, 1, 3, 0, None):
+        if slot is not None and slot < 4:
+            wait_bytes(quad_sib.at[slot], qs_recv.at[slot])
+        both_later = None if later is None else product(later)
+        if slot is not None:
+            part = terms(slot, both)
+            if slot < 4:
+                part = part + quad_sib[slot]
             quad[slot * OWN : (slot + 1) * OWN, :] = part
-            send(
-                quad_slot(slot), quad_sib.at[slot - 4], x_send.at[6], qs_recv.at[slot - 4],
-                peer(dc=1),
-            )
-            continue
-        wait_bytes(quad_sib.at[slot], qs_recv.at[slot])
-        quad[slot * OWN : (slot + 1) * OWN, :] = part + quad_sib[slot]
-        if slot:
-            to = (-slot) % 4
-            send(quad_slot(slot), quad_ring.at[to], x_send.at[7], qr_recv.at[to], peer(dx=slot))
+            if slot > 3:
+                send(
+                    quad_slot(slot), quad_sib.at[slot - 4], x_send.at[6], qs_recv.at[slot - 4],
+                    peer(dc=1),
+                )
+            elif slot > 0:
+                to = (-slot) % 4
+                send(quad_slot(slot), quad_ring.at[to], x_send.at[7], qr_recv.at[to], peer(dx=slot))
+        slot, both = later, both_later
 
     summed = quad[0:OWN, :]
     for d in (1, 3, 2):
@@ -407,18 +417,18 @@
     )
     wait_bytes(feat_sib, feat_recv.at[0])
     wait_bytes(dz_sib, dz_recv.at[0])
-    grad[...] += lax.dot_general(feat_sib[...], dz_sib[...], TN, preferred_element_type=F32)
-
     g1_in, g1, g2_in = (g1_in_a, g1_in_b, g1_in_c), (g1_a, g1_b, g1_c), (g2_in_a, g2_in_b, g2_in_c)
-    parts = (2, 1, 0)
+    parts = (0, 1, 2)
 
     def ring_block(part, d, base=0):
         span = 16 * TILES[part]
         first = base + STARTS[part] + torus.ring_at(part, d) * span
         return pl.ds(pl.multiple_of(first, span), span)
 
-    for d in (2, 1, 3):
-        for part in parts:
+    for part in parts:
+        of = slice(STARTS[part], STARTS[part] + 64 * TILES[part])
+        grad[of, :] += lax.dot_general(feat_sib[:, of], dz_sib[...], TN, preferred_element_type=F32)
+        for d in (2, 1, 3):
             at = (-d) % 4
             send(
                 grad.at[ring_block(part, d)], g1_in[part].at[at],
@@ -470,9 +480,6 @@
                 torus.plane_peer(part, d1, d2),
             )
 
-    def store(rows_of):
-        pltpu.make_async_copy(out.at[rows_of], g_ref.at[rows_of], store_sem.at[0]).start()
-
     for part in parts:
         wait_bytes(out.at[pl.ds(0, 15 * TILES[part])], ag_recv.at[part])
         block = ring_block(part, 0, base)
@@ -483,13 +490,11 @@
                 torus.ring_peer(part, d),
             )
         send(out.at[block], out.at[block], x_send.at[14], rel_recv.at[part, 0], peer(dc=1))
-        store(block)
     for d in (1, 3, 2):
         for part in parts:
             block = ring_block(part, d, base)
             wait_bytes(out.at[block], ring_recv.at[part, d])
             send(out.at[block], out.at[block], x_send.at[14], rel_recv.at[part, d], peer(dc=1))
-            store(block)
 
     for slot in range(1, 16):
         wait_bytes(loss2.at[0], loss_recv2.at[slot])
@@ -506,11 +511,9 @@
             ring = torus.zs[d] if part == 2 else torus.pick(*(ends if part == 0 else ends[::-1]))
             block = pl.ds(pl.multiple_of(other + STARTS[part] + ring * span, span), span)
             wait_bytes(out.at[block], rel_recv.at[part, d])
-            store(block)
 
     for ref, at in sent:
         wait_bytes(ref, x_send.at[at])
-    wait_bytes(out, store_sem.at[0])
 
 
 def per_device(features, proj_weight, partner):
@@ -519,15 +522,16 @@
         kernel,
         out_shape=(
             pltpu.VMEM((D, PROJ), F32),
-            jax.ShapeDtypeStruct((1, 1), F32),
+            pltpu.VMEM((1, 1), F32),
         ),
         in_specs=[
             pl.BlockSpec(memory_space=pl.ANY),
             pl.BlockSpec(memory_space=pl.ANY),
-            pl.BlockSpec(memory_space=pltpu.VMEM),
+            pl.BlockSpec(memory_space=pl.ANY),
         ],
         out_specs=(pl.BlockSpec(memory_space=pltpu.VMEM), pl.BlockSpec(memory_space=pltpu.VMEM)),
         scratch_shapes=[
+            pltpu.VMEM((2, PROJ), jnp.int32),
             pltpu.VMEM((OWN, D), BF16),
             pltpu.VMEM((D, PROJ), BF16),
             pltpu.VMEM((OWN, HALF), BF16),
@@ -553,10 +557,9 @@
             *[pltpu.VMEM((4, 16 * tile, PROJ), F32) for tile in TILES],
             *[pltpu.VMEM((16 * tile, PROJ), F32) for tile in TILES],
             *[pltpu.VMEM((16 * tile, PROJ), F32) for tile in TILES],
-            pltpu.VMEM((D, PROJ), F32),
             pltpu.VMEM((8, 8, PROJ), F32),
             pltpu.VMEM((16, 8, PROJ), F32),
-            dma((8,)),
+            dma((9,)),
             dma((15,)),
             dma((16, 2)),
             dma((8,)),
@@ -573,7 +576,6 @@
             dma((3,)),
             dma((3, 4)),
             dma((3, 4)),
-            dma((1,)),
         ],
         compiler_params=pltpu.CompilerParams(
             collective_id=0, has_side_effects=True, vmem_limit_bytes=56 * 2**20

time: 75.7 us -> 72.7 us (0.960)
  Pallas kernels: 71.9 us -> 69.5 us
    pallas_call x1, Pallas kernels: 71.9 us -> 69.5 us  [per_device(): pl.pallas_call(kernel, out_shape=(pltpu.VMEM((D, PROJ), F32), pltpu.VMEM(...]
where the time goes in v4:
time: 72.7 us; the launch traced here: 72.6 us
  Pallas kernels  69.5 us (96%)
  between operations  1.8 us (2%)
  local copies, waits for them, and re-layouts  1.32 us (2%)
    pallas_call x1, Pallas kernels, per_device(): pl.pallas_call(kernel, out_shape=(pltpu.VMEM((D, PROJ), F32), pltpu.VMEM(...  69.5 us

profile of v4, /device:TPU:1, one launch (start us, length us, event | category | flops | bytes accessed | tf_op | source)
XLA Modules:
  0.0 72.6 jit_solution(8353289892825708830)
XLA Ops:
  0.6 69.5 %simclr_head.1 = (f32[4096,128]{1,0:T(8,128)S(1)}, f32[1,1]{1,0:T(1,128)S(1)}) custom-call(bf16[256,4096]{1,0:T(8,128)(2,1)} %f_hbm.1, bf16[4096,128]{1,0:T(8,128)(2,1)} %w_hbm.1, s32[2,128]{1,0:T(2,128)} %bitcast.2), custom_call_target="tpu_custom_call" | custom-call | tf_op jit(solution)/shard_map/simclr_head/pallas_call | solution.py:521
  70.2 1.3 %copy.8 = f32[4096,128]{1,0:T(8,128)} copy(f32[4096,128]{1,0:T(8,128)S(1)} %get-tuple-element.7) | data formatting | bytes 4194304

commit v5 on v4

--- a/solution.py
+++ b/solution.py
@@ -14,7 +14,8 @@
 QUARTER = D // 4
 PROJ = 128
 OWN = 256
-GROUPS = ((0, 4), (4, 8), (8, 12), (12, 14), (14, 16))
+RINGS = 7
+GROUPS = ((RINGS, 11), (11, 14), (14, 16))
 SLOT = OWN + 16
 INV_TAU = 5.0
 SCALE2 = INV_TAU * 1.4426950408889634
@@ -229,15 +230,6 @@
         wait_bytes(row_slot(slot), row_recv.at[slot])
         send(row_slot(slot), row_slot(4 + slot), x_send.at[0], row_recv.at[4 + slot], peer(dc=1))
 
-    for d in (1, 3, 2):
-        pass_on(0, d)
-        pass_on(1, d)
-        pass_row(d)
-    send(
-        feat.at[:, pl.ds(pl.multiple_of((1 - c) * HALF, HALF), HALF)], feat_sib,
-        x_send.at[2], feat_recv.at[0], peer(dc=1),
-    )
-
     def lanes(e):
         total = e[:, 0:PROJ]
         for q in range(1, e.shape[1] // PROJ):
@@ -253,28 +245,53 @@
             * SCALE2
         )
 
-    for slot in range(1, 4):
-        wait_bytes(col_half(slot, 1 - RING_AXIS[slot]), col_recv.at[slot, 1 - RING_AXIS[slot]])
-    for slot in (0, 4, 1, 3, 2, 5, 7, 6):
-        if slot > 3:
-            wait_bytes(row_slot(slot), row_recv.at[slot])
-        e = scores(slot, *GROUPS[0])
-        if slot == 0:
+    def pass1(slot, first, end):
+        e = scores(slot, first, end)
+        if slot == 0 and first == 0:
             at_row = lax.broadcasted_iota(jnp.int32, e.shape, 0)
             at_col = lax.broadcasted_iota(jnp.int32, e.shape, 1)
             e = jnp.where(at_row == at_col, 0.0, e)
-        expo[slot * OWN : (slot + 1) * OWN, 0 : GROUPS[0][1] * OWN] = e.astype(BF16)
-        acc[slot * OWN : (slot + 1) * OWN, :] = lanes(e)
-
-    for first, end in GROUPS[1:]:
+        of = slice(slot * OWN, (slot + 1) * OWN)
+        expo[of, first * OWN : end * OWN] = e.astype(BF16)
+        if first == 0:
+            acc[of, :] = lanes(e)
+        else:
+            acc[of, :] += lanes(e)
+
+    def wait_ring(slot):
+        half = 1 - RING_AXIS[slot]
+        wait_bytes(col_half(slot, half), col_recv.at[slot, half])
+
+    for d in (1, 3):
+        pass_on(0, d)
+        pass_on(1, d)
+        pass_row(d)
+    pass_on(0, 2)
+    pass_on(1, 2)
+    wait_bytes(row_slot(4), row_recv.at[4])
+    for slot in range(1, 4):
+        wait_ring(slot)
+    for slot in (0, 4, 1, 3):
+        pass1(slot, 0, 4)
+    pass_row(2)
+    send(
+        feat.at[:, pl.ds(pl.multiple_of((1 - c) * HALF, HALF), HALF)], feat_sib,
+        x_send.at[2], feat_recv.at[0], peer(dc=1),
+    )
+    for slot in range(4, RINGS):
+        wait_ring(slot)
+    for slot in (0, 4, 1, 3):
+        pass1(slot, 4, RINGS)
+    for slot in (5, 7, 6):
+        wait_bytes(row_slot(slot), row_recv.at[slot])
+    for slot in (5, 7, 2, 6):
+        pass1(slot, 0, RINGS)
+    for first, end in GROUPS:
         for slot in range(first, end):
             for half in range(2):
-                if slot not in RING_AXIS or half != RING_AXIS[slot]:
-                    wait_bytes(col_half(slot, half), col_recv.at[slot, half])
+                wait_bytes(col_half(slot, half), col_recv.at[slot, half])
         for slot in range(8):
-            e = scores(slot, first, end)
-            expo[slot * OWN : (slot + 1) * OWN, first * OWN : end * OWN] = e.astype(BF16)
-            acc[slot * OWN : (slot + 1) * OWN, :] += lanes(e)
+            pass1(slot, first, end)
 
     eye = lax.broadcasted_iota(jnp.int32, (PROJ, PROJ), 0) == lax.broadcasted_iota(
         jnp.int32, (PROJ, PROJ), 1
@@ -283,10 +300,9 @@
     def to_row(column):
         return jnp.sum(jnp.where(eye, column, 0.0), axis=0, keepdims=True)
 
-    def to_column(row):
+    def to_column(*rows_of):
         halves = [
-            jnp.sum(jnp.where(eye, row[:, h * PROJ : (h + 1) * PROJ], 0.0), axis=1, keepdims=True)
-            for h in range(2)
+            jnp.sum(jnp.where(eye, row, 0.0), axis=1, keepdims=True) for row in rows_of
         ]
         return jnp.broadcast_to(jnp.concatenate(halves, axis=0), (OWN, PROJ))
 
@@ -301,13 +317,15 @@
         send(sums, sums_in.at[to], x_send.at[3], sum_recv.at[to], peer(dx=dx, dc=dc))
 
     for slot in range(16):
-        wide[:, slot * PROJ : (slot + 1) * PROJ] = cols[slot * OWN : (slot + 1) * OWN, :]
+        block = cols[slot * OWN : (slot + 1) * OWN, :]
+        wide[:, slot * PROJ : (slot + 1) * PROJ] = block
+        uw[slot * OWN : (slot + 1) * OWN, 0:PROJ] = block
     lane = lax.broadcasted_iota(jnp.int32, (OWN, PROJ), 1).astype(F32)
 
     def partners(slot, pos):
         code = rows[slot * SLOT + OWN : (slot + 1) * SLOT, :].astype(F32)
-        owner = to_column(jnp.concatenate([code[0:1], code[1:2]], axis=1))
-        place = to_column(jnp.concatenate([code[2:3], code[3:4]], axis=1))
+        owner = to_column(code[0:1], code[1:2])
+        place = to_column(code[2:3], code[3:4])
         hot = jnp.concatenate(
             [jnp.where(place == lane, 1.0, 0.0), jnp.where(place == lane + PROJ, 1.0, 0.0)], axis=1
         ).astype(BF16)
@@ -335,35 +353,36 @@
             ox, oc = ROW_OFFS[sender]
             at = ROW_OF[((dx - ox) % 4, (dc - oc) % 2)]
             total = total + sums_in[sender, at : at + 1, :]
-        wts[slot : slot + 1, :] = 1.0 / total
+        for h in range(2):
+            wts[slot, h : h + 1, :] = 1.0 / total[:, h * PROJ : (h + 1) * PROJ]
         if slot == 0:
             log_sum = jnp.sum(jnp.log(total))
     for slot in range(1, 16):
         dy, dz = COL_OFFS[slot]
         to = COL_OF[neg_col((dy, dz))]
-        send(wts, wts_in.at[to], x_send.at[4], wt_recv.at[to], peer(dy=dy, dz=dz))
+        send(wts.at[0], wts_in.at[to], x_send.at[4], wt_recv.at[to], peer(dy=dy, dz=dz))
 
     for slot in range(4, 8):
         pos = partners(slot, pos)
     loss_part = log_sum - INV_TAU * jnp.sum(pos)
     me1 = x * 2 + c
-    loss1[me1] = jnp.full((8, PROJ), loss_part, F32)
+    loss1[me1] = jnp.full((1, PROJ), loss_part, F32)
     for slot in range(1, 8):
         dx, dc = ROW_OFFS[slot]
         to = ROW_OF[neg_row((dx, dc))]
         send(loss1.at[me1], loss1.at[me1], x_send.at[5], loss_recv1.at[to], peer(dx=dx, dc=dc))
 
-    def weigh(slot, row):
+    def weigh(slot, table):
         block = cols[slot * OWN : (slot + 1) * OWN, :]
-        uw[slot * OWN : (slot + 1) * OWN, 0:PROJ] = block
         uw[slot * OWN : (slot + 1) * OWN, PROJ : 2 * PROJ] = (
-            block.astype(F32) * to_column(row)
+            block.astype(F32) * to_column(table[0:1], table[1:2])
         ).astype(BF16)
 
-    weigh(0, wts[0:1, :])
+    weigh(0, wts[0])
     for slot in range(1, 16):
         wait_bytes(wts_in.at[slot], wt_recv.at[slot])
-        weigh(slot, wts_in[slot, 0:1, :])
+    for slot in range(1, 16):
+        weigh(slot, wts_in[slot])
 
     def product(slot):
         return jnp.dot(
@@ -371,7 +390,7 @@
         )
 
     def terms(slot, both):
-        w = to_column(wts[slot : slot + 1, :])
+        w = to_column(wts[slot, 0:1, :], wts[slot, 1:2, :])
         return (
             w * both[:, 0:PROJ] + both[:, PROJ : 2 * PROJ]
             - 2.0 * paired[slot * OWN : (slot + 1) * OWN, :]
@@ -418,14 +437,14 @@
     wait_bytes(feat_sib, feat_recv.at[0])
     wait_bytes(dz_sib, dz_recv.at[0])
     g1_in, g1, g2_in = (g1_in_a, g1_in_b, g1_in_c), (g1_a, g1_b, g1_c), (g2_in_a, g2_in_b, g2_in_c)
-    parts = (0, 1, 2)
+    parts = (2, 1, 0)
 
     def ring_block(part, d, base=0):
         span = 16 * TILES[part]
         first = base + STARTS[part] + torus.ring_at(part, d) * span
         return pl.ds(pl.multiple_of(first, span), span)
 
-    for part in parts:
+    for part in (0, 1, 2):
         of = slice(STARTS[part], STARTS[part] + 64 * TILES[part])
         grad[of, :] += lax.dot_general(feat_sib[:, of], dz_sib[...], TN, preferred_element_type=F32)
         for d in (2, 1, 3):
@@ -543,8 +562,8 @@
             pltpu.VMEM((8 * OWN, PROJ), F32),
             pltpu.VMEM((8, OWN), F32),
             pltpu.VMEM((8, 8, OWN), F32),
-            pltpu.VMEM((8, OWN), F32),
-            pltpu.VMEM((16, 8, OWN), F32),
+            pltpu.VMEM((8, 2, PROJ), F32),
+            pltpu.VMEM((16, 2, PROJ), F32),
             pltpu.VMEM((OWN, 16 * PROJ), BF16),
             pltpu.VMEM((8 * OWN, PROJ), F32),
             pltpu.VMEM((16 * OWN, 2 * PROJ), BF16),
@@ -557,8 +576,8 @@
             *[pltpu.VMEM((4, 16 * tile, PROJ), F32) for tile in TILES],
             *[pltpu.VMEM((16 * tile, PROJ), F32) for tile in TILES],
             *[pltpu.VMEM((16 * tile, PROJ), F32) for tile in TILES],
-            pltpu.VMEM((8, 8, PROJ), F32),
-            pltpu.VMEM((16, 8, PROJ), F32),
+            pltpu.VMEM((8, 1, PROJ), F32),
+            pltpu.VMEM((16, 1, PROJ), F32),
             dma((9,)),
             dma((15,)),
             dma((16, 2)),

time: 72.7 us -> 70.9 us (0.975)
  Pallas kernels: 69.5 us -> 67.6 us
    pallas_call x1, Pallas kernels: 69.5 us -> 67.6 us  [per_device(): pl.pallas_call(kernel, out_shape=(pltpu.VMEM((D, PROJ), F32), pltpu.VMEM(...]
where the time goes in v5:
time: 70.9 us; the launch traced here: 70.8 us
  Pallas kernels  67.6 us (95%)
  between operations  1.8 us (3%)
  local copies, waits for them, and re-layouts  1.32 us (2%)
    pallas_call x1, Pallas kernels, per_device(): pl.pallas_call(kernel, out_shape=(pltpu.VMEM((D, PROJ), F32), pltpu.VMEM(...  67.6 us

profile of v5, /device:TPU:1, one launch (start us, length us, event | category | flops | bytes accessed | tf_op | source)
XLA Modules:
  0.0 70.8 jit_solution(14348383051564070819)
XLA Ops:
  0.6 67.6 %simclr_head.1 = (f32[4096,128]{1,0:T(8,128)S(1)}, f32[1,1]{1,0:T(1,128)S(1)}) custom-call(bf16[256,4096]{1,0:T(8,128)(2,1)} %f_hbm.1, bf16[4096,128]{1,0:T(8,128)(2,1)} %w_hbm.1, s32[2,128]{1,0:T(2,128)} %bitcast.2), custom_call_target="tpu_custom_call" | custom-call | tf_op jit(solution)/shard_map/simclr_head/pallas_call | solution.py:540
  68.3 1.3 %copy.8 = f32[4096,128]{1,0:T(8,128)} copy(f32[4096,128]{1,0:T(8,128)S(1)} %get-tuple-element.7) | data formatting | bytes 4194304

commit v6 on v5

--- a/solution.py
+++ b/solution.py
@@ -80,6 +80,12 @@
         ends = (self.xs[d], self.ys[d])
         return self.pick(*(ends if part == 0 else ends[::-1]))
 
+    def row_at(self, part, d1):
+        if part == 2:
+            return self.xs[d1]
+        ends = (self.ys[d1], self.xs[d1])
+        return self.pick(*(ends if part == 0 else ends[::-1]))
+
     def plane_at(self, part, d1, d2):
         if part == 2:
             return self.xs[d1] * 4 + self.ys[d2]
@@ -119,7 +125,7 @@
 def kernel(
     f_hbm, w_hbm, partner_hbm, out, loss_ref,
     partner_ref, feat, weight, feat_sib, u_ref, norm_ref, rows, cols, expo, acc,
-    sums, sums_in, wts, wts_in, wide, paired, uw, quad, quad_sib, quad_ring,
+    sums, sums_in, wts, wts_in, wide, paired, uw, w_rows, quad, quad_sib, quad_ring,
     dz_own, dz_sib, grad, g1_in_a, g1_in_b, g1_in_c, g1_a, g1_b, g1_c,
     g2_in_a, g2_in_b, g2_in_c, loss1, loss2,
     load_sem, x_send, col_recv, row_recv, feat_recv, sum_recv, wt_recv, loss_recv1, loss_recv2,
@@ -364,6 +370,8 @@
 
     for slot in range(4, 8):
         pos = partners(slot, pos)
+    for slot in range(8):
+        w_rows[slot * OWN : (slot + 1) * OWN, :] = to_column(wts[slot, 0:1, :], wts[slot, 1:2, :])
     loss_part = log_sum - INV_TAU * jnp.sum(pos)
     me1 = x * 2 + c
     loss1[me1] = jnp.full((1, PROJ), loss_part, F32)
@@ -390,7 +398,7 @@
         )
 
     def terms(slot, both):
-        w = to_column(wts[slot, 0:1, :], wts[slot, 1:2, :])
+        w = w_rows[slot * OWN : (slot + 1) * OWN, :]
         return (
             w * both[:, 0:PROJ] + both[:, PROJ : 2 * PROJ]
             - 2.0 * paired[slot * OWN : (slot + 1) * OWN, :]
@@ -399,25 +407,34 @@
     def quad_slot(slot):
         return quad.at[pl.ds(slot * OWN, OWN)]
 
-    slot, both = None, None
-    for later in (6, 5, 7, 2, 4, 1, 3, 0, None):
-        if slot is not None and slot < 4:
-            wait_bytes(quad_sib.at[slot], qs_recv.at[slot])
-        both_later = None if later is None else product(later)
+    def finish(slot, both):
+        quad[slot * OWN : (slot + 1) * OWN, :] = terms(slot, both)
+        if slot > 3:
+            send(
+                quad_slot(slot), quad_sib.at[slot - 4], x_send.at[6], qs_recv.at[slot - 4],
+                peer(dc=1),
+            )
+
+    def complete(slot):
+        quad[slot * OWN : (slot + 1) * OWN, :] += quad_sib[slot]
+        if slot:
+            to = (-slot) % 4
+            send(quad_slot(slot), quad_ring.at[to], x_send.at[7], qr_recv.at[to], peer(dx=slot))
+
+    slot, both, ready = None, None, None
+    for later in (6, 2, 5, 1, 7, 3, 4, 0):
+        if ready is not None:
+            wait_bytes(quad_sib.at[ready], qs_recv.at[ready])
+        both_later = product(later)
+        if ready is not None:
+            complete(ready)
         if slot is not None:
-            part = terms(slot, both)
-            if slot < 4:
-                part = part + quad_sib[slot]
-            quad[slot * OWN : (slot + 1) * OWN, :] = part
-            if slot > 3:
-                send(
-                    quad_slot(slot), quad_sib.at[slot - 4], x_send.at[6], qs_recv.at[slot - 4],
-                    peer(dc=1),
-                )
-            elif slot > 0:
-                to = (-slot) % 4
-                send(quad_slot(slot), quad_ring.at[to], x_send.at[7], qr_recv.at[to], peer(dx=slot))
+            finish(slot, both)
+        ready = slot if slot is not None and slot < 4 else None
         slot, both = later, both_later
+    finish(slot, both)
+    wait_bytes(quad_sib.at[slot], qs_recv.at[slot])
+    complete(slot)
 
     summed = quad[0:OWN, :]
     for d in (1, 3, 2):
@@ -444,15 +461,25 @@
         first = base + STARTS[part] + torus.ring_at(part, d) * span
         return pl.ds(pl.multiple_of(first, span), span)
 
+    def block_row(part, d1):
+        span = 4 * TILES[part]
+        return pl.ds(pl.multiple_of(torus.row_at(part, d1) * span, span), span)
+
+    def plane_row(part, d, d1, base=0):
+        span = 4 * TILES[part]
+        first = base + STARTS[part] + torus.ring_at(part, d) * 4 * span
+        return pl.ds(pl.multiple_of(first + torus.row_at(part, d1) * span, span), span)
+
     for part in (0, 1, 2):
         of = slice(STARTS[part], STARTS[part] + 64 * TILES[part])
         grad[of, :] += lax.dot_general(feat_sib[:, of], dz_sib[...], TN, preferred_element_type=F32)
-        for d in (2, 1, 3):
-            at = (-d) % 4
-            send(
-                grad.at[ring_block(part, d)], g1_in[part].at[at],
-                x_send.at[10], g1_recv.at[part, at], torus.ring_peer(part, d),
-            )
+        for d1 in (2, 1, 3, 0):
+            for d in (2, 1, 3):
+                at = (-d) % 4
+                send(
+                    grad.at[plane_row(part, d, d1)], g1_in[part].at[at, block_row(part, d1)],
+                    x_send.at[10], g1_recv.at[part, at, d1], torus.ring_peer(part, d),
+                )
 
     for slot in range(1, 8):
         wait_bytes(loss1.at[0], loss_recv1.at[slot])
@@ -466,21 +493,24 @@
         to = COL_OF[neg_col((dy, dz))]
         send(loss2.at[me2], loss2.at[me2], x_send.at[8], loss_recv2.at[to], peer(dy=dy, dz=dz))
 
-    for part in parts:
-        total = grad[ring_block(part, 0), :]
-        for d in (1, 3, 2):
-            wait_bytes(g1_in[part].at[d], g1_recv.at[part, d])
-            total = total + g1_in[part][d]
-        g1[part][...] = total
-        tile = TILES[part]
-        for slot in range(15, 0, -1):
-            d1, d2 = COL_OFFS[slot]
-            to = COL_OF[neg_col((d1, d2))]
-            at = pl.multiple_of(torus.plane_at(part, d1, d2) * tile, tile)
-            send(
-                g1[part].at[pl.ds(at, tile)], g2_in[part].at[pl.ds(to * tile, tile)],
-                x_send.at[11], g2_recv.at[part], torus.plane_peer(part, d1, d2),
-            )
+    for d1 in (2, 1, 3, 0):
+        for part in parts:
+            rows_of = block_row(part, d1)
+            total = grad[plane_row(part, 0, d1), :]
+            for d in (1, 3, 2):
+                wait_bytes(g1_in[part].at[d, rows_of], g1_recv.at[part, d, d1])
+                total = total + g1_in[part][d, rows_of, :]
+            g1[part][rows_of, :] = total
+            tile = TILES[part]
+            for d2 in (2, 1, 3, 0):
+                if not (d1 or d2):
+                    continue
+                to = COL_OF[neg_col((d1, d2))]
+                at = pl.multiple_of(torus.plane_at(part, d1, d2) * tile, tile)
+                send(
+                    g1[part].at[pl.ds(at, tile)], g2_in[part].at[pl.ds(to * tile, tile)],
+                    x_send.at[11], g2_recv.at[part], torus.plane_peer(part, d1, d2),
+                )
     base = c * HALF
     for part in parts:
         tile = TILES[part]
@@ -495,25 +525,28 @@
         for slot in range(15, 0, -1):
             d1, d2 = COL_OFFS[slot]
             send(
-                out.at[at], out.at[at], x_send.at[12], ag_recv.at[part],
+                out.at[at], out.at[at], x_send.at[12], ag_recv.at[part, (-d1) % 4],
                 torus.plane_peer(part, d1, d2),
             )
 
+    for d1 in (0, 1, 3, 2):
+        for part in parts:
+            wait_bytes(out.at[pl.ds(0, (4 if d1 else 3) * TILES[part])], ag_recv.at[part, d1])
+            block = plane_row(part, 0, d1, base)
+            for d in (2, 1, 3):
+                send(
+                    out.at[block], out.at[block], x_send.at[13],
+                    ring_recv.at[part, (-d) % 4, d1], torus.ring_peer(part, d),
+                )
     for part in parts:
-        wait_bytes(out.at[pl.ds(0, 15 * TILES[part])], ag_recv.at[part])
         block = ring_block(part, 0, base)
-        for d in (2, 1, 3):
-            at = (-d) % 4
-            send(
-                out.at[block], out.at[block], x_send.at[13], ring_recv.at[part, at],
-                torus.ring_peer(part, d),
-            )
         send(out.at[block], out.at[block], x_send.at[14], rel_recv.at[part, 0], peer(dc=1))
-    for d in (1, 3, 2):
-        for part in parts:
-            block = ring_block(part, d, base)
-            wait_bytes(out.at[block], ring_recv.at[part, d])
-            send(out.at[block], out.at[block], x_send.at[14], rel_recv.at[part, d], peer(dc=1))
+    for d1 in (0, 1, 3, 2):
+        for d in (1, 3, 2):
+            for part in parts:
+                block = plane_row(part, d, d1, base)
+                wait_bytes(out.at[block], ring_recv.at[part, d, d1])
+                send(out.at[block], out.at[block], x_send.at[14], rel_recv.at[part, d], peer(dc=1))
 
     for slot in range(1, 16):
         wait_bytes(loss2.at[0], loss_recv2.at[slot])
@@ -568,6 +601,7 @@
             pltpu.VMEM((8 * OWN, PROJ), F32),
             pltpu.VMEM((16 * OWN, 2 * PROJ), BF16),
             pltpu.VMEM((8 * OWN, PROJ), F32),
+            pltpu.VMEM((8 * OWN, PROJ), F32),
             pltpu.VMEM((4, OWN, PROJ), F32),
             pltpu.VMEM((4, OWN, PROJ), F32),
             pltpu.VMEM((OWN, PROJ), BF16),
@@ -590,10 +624,10 @@
             dma((4,)),
             dma((4,)),
             dma((1,)),
-            dma((3, 4)),
-            dma((3,)),
+            dma((3, 4, 4)),
             dma((3,)),
             dma((3, 4)),
+            dma((3, 4, 4)),
             dma((3, 4)),
         ],
         compiler_params=pltpu.CompilerParams(

time: 70.9 us -> 69.3 us (0.977)
  Pallas kernels: 67.6 us -> 66 us
    pallas_call x1, Pallas kernels: 67.6 us -> 66 us  [per_device(): pl.pallas_call(kernel, out_shape=(pltpu.VMEM((D, PROJ), F32), pltpu.VMEM(...]
where the time goes in v6:
time: 69.3 us; the launch traced here: 69.1 us
  Pallas kernels  66 us (95%)
  between operations  1.8 us (3%)
  local copies, waits for them, and re-layouts  1.32 us (2%)
    pallas_call x1, Pallas kernels, per_device(): pl.pallas_call(kernel, out_shape=(pltpu.VMEM((D, PROJ), F32), pltpu.VMEM(...  66 us

profile of v6, /device:TPU:1, one launch (start us, length us, event | category | flops | bytes accessed | tf_op | source)
XLA Modules:
  0.0 69.1 jit_solution(3105653524674880680)
XLA Ops:
  0.6 66.0 %simclr_head.1 = (f32[4096,128]{1,0:T(8,128)S(1)}, f32[1,1]{1,0:T(1,128)S(1)}) custom-call(bf16[256,4096]{1,0:T(8,128)(2,1)} %f_hbm.1, bf16[4096,128]{1,0:T(8,128)(2,1)} %w_hbm.1, s32[2,128]{1,0:T(2,128)} %bitcast.2), custom_call_target="tpu_custom_call" | custom-call | tf_op jit(solution)/shard_map/simclr_head/pallas_call | solution.py:573
  66.7 1.3 %copy.8 = f32[4096,128]{1,0:T(8,128)} copy(f32[4096,128]{1,0:T(8,128)S(1)} %get-tuple-element.7) | data formatting | bytes 4194304

commit v7 on v6

--- a/solution.py
+++ b/solution.py
@@ -421,20 +421,25 @@
             to = (-slot) % 4
             send(quad_slot(slot), quad_ring.at[to], x_send.at[7], qr_recv.at[to], peer(dx=slot))
 
-    slot, both, ready = None, None, None
-    for later in (6, 2, 5, 1, 7, 3, 4, 0):
-        if ready is not None:
-            wait_bytes(quad_sib.at[ready], qs_recv.at[ready])
+    def add_sibling(slot):
+        wait_bytes(quad_sib.at[slot], qs_recv.at[slot])
+        complete(slot)
+
+    finish(6, product(6))
+    finish(2, product(2))
+    add_sibling(2)
+    slot, both = 5, product(5)
+    for later in (7, 1, 3):
         both_later = product(later)
-        if ready is not None:
-            complete(ready)
-        if slot is not None:
-            finish(slot, both)
-        ready = slot if slot is not None and slot < 4 else None
+        finish(slot, both)
         slot, both = later, both_later
-    finish(slot, both)
-    wait_bytes(quad_sib.at[slot], qs_recv.at[slot])
-    complete(slot)
+    add_sibling(1)
+    finish(3, both)
+    add_sibling(3)
+    both, both_later = product(4), product(0)
+    finish(4, both)
+    finish(0, both_later)
+    add_sibling(0)
 
     summed = quad[0:OWN, :]
     for d in (1, 3, 2):

time: 69.3 us -> 68.5 us (0.988)
  Pallas kernels: 66 us -> 65.2 us
    pallas_call x1, Pallas kernels: 66 us -> 65.2 us  [per_device(): pl.pallas_call(kernel, out_shape=(pltpu.VMEM((D, PROJ), F32), pltpu.VMEM(...]
where the time goes in v7:
time: 68.5 us; the launch traced here: 68.3 us
  Pallas kernels  65.2 us (95%)
  between operations  1.8 us (3%)
  local copies, waits for them, and re-layouts  1.32 us (2%)
    pallas_call x1, Pallas kernels, per_device(): pl.pallas_call(kernel, out_shape=(pltpu.VMEM((D, PROJ), F32), pltpu.VMEM(...  65.2 us

profile of v7, /device:TPU:1, one launch (start us, length us, event | category | flops | bytes accessed | tf_op | source)
XLA Modules:
  0.0 68.3 jit_solution(7053726434325115750)
XLA Ops:
  0.6 65.2 %simclr_head.1 = (f32[4096,128]{1,0:T(8,128)S(1)}, f32[1,1]{1,0:T(1,128)S(1)}) custom-call(bf16[256,4096]{1,0:T(8,128)(2,1)} %f_hbm.1, bf16[4096,128]{1,0:T(8,128)(2,1)} %w_hbm.1, s32[2,128]{1,0:T(2,128)} %bitcast.2), custom_call_target="tpu_custom_call" | custom-call | tf_op jit(solution)/shard_map/simclr_head/pallas_call | solution.py:578
  65.9 1.3 %copy.8 = f32[4096,128]{1,0:T(8,128)} copy(f32[4096,128]{1,0:T(8,128)S(1)} %get-tuple-element.7) | data formatting | bytes 4194304

commit v8 on v7

--- a/solution.py
+++ b/solution.py
@@ -160,16 +160,16 @@
                 pltpu.make_async_copy(f_hbm.at[:, depth], feat.at[:, depth], load_sem.at[4 + k]),
             )
         )
+    barrier = pltpu.get_barrier_semaphore()
+    peers = ring_peers()
+    for off in peers:
+        pl.semaphore_signal(barrier, inc=1, device_id=peer(*off), device_id_type=MESH)
+
     load_partner = pltpu.make_async_copy(partner_hbm, partner_ref, load_sem.at[8])
     load_partner.start()
     for pair in loads:
         for load in pair:
             load.start()
-    barrier = pltpu.get_barrier_semaphore()
-    peers = ring_peers()
-    for off in peers:
-        pl.semaphore_signal(barrier, inc=1, device_id=peer(*off), device_id_type=MESH)
-
     load_partner.wait()
     owner_of, place_of = partner_ref[...] // OWN, partner_ref[...] % OWN
     at = lax.broadcasted_iota(jnp.int32, (16, PROJ), 0)
@@ -486,18 +486,6 @@
                     x_send.at[10], g1_recv.at[part, at, d1], torus.ring_peer(part, d),
                 )
 
-    for slot in range(1, 8):
-        wait_bytes(loss1.at[0], loss_recv1.at[slot])
-    total = loss1[0]
-    for k in range(1, 8):
-        total = total + loss1[k]
-    me2 = y * 4 + z
-    loss2[me2] = total
-    for slot in range(1, 16):
-        dy, dz = COL_OFFS[slot]
-        to = COL_OF[neg_col((dy, dz))]
-        send(loss2.at[me2], loss2.at[me2], x_send.at[8], loss_recv2.at[to], peer(dy=dy, dz=dz))
-
     for d1 in (2, 1, 3, 0):
         for part in parts:
             rows_of = block_row(part, d1)
@@ -516,6 +504,18 @@
                     g1[part].at[pl.ds(at, tile)], g2_in[part].at[pl.ds(to * tile, tile)],
                     x_send.at[11], g2_recv.at[part], torus.plane_peer(part, d1, d2),
                 )
+    for slot in range(1, 8):
+        wait_bytes(loss1.at[0], loss_recv1.at[slot])
+    total = loss1[0]
+    for k in range(1, 8):
+        total = total + loss1[k]
+    me2 = y * 4 + z
+    loss2[me2] = total
+    for slot in range(1, 16):
+        dy, dz = COL_OFFS[slot]
+        to = COL_OF[neg_col((dy, dz))]
+        send(loss2.at[me2], loss2.at[me2], x_send.at[8], loss_recv2.at[to], peer(dy=dy, dz=dz))
+
     base = c * HALF
     for part in parts:
         tile = TILES[part]
@@ -527,7 +527,7 @@
         first = base + STARTS[part] + torus.ring_at(part, 0) * 16 * tile + place
         at = pl.ds(pl.multiple_of(first, tile), tile)
         out[at, :] = total * (1.0 / VIEWS**0.5)
-        for slot in range(15, 0, -1):
+        for slot in sorted(range(1, 16), key=lambda k: (COL_OFFS[k][0] != 0, -k)):
             d1, d2 = COL_OFFS[slot]
             send(
                 out.at[at], out.at[at], x_send.at[12], ag_recv.at[part, (-d1) % 4],

time: 68.5 us -> 68.1 us (level)
  no operation moved by 1% of the time
where the time goes in v8:
time: 68.1 us; the launch traced here: 68 us
  Pallas kernels  64.9 us (95%)
  between operations  1.8 us (3%)
  local copies, waits for them, and re-layouts  1.32 us (2%)
    pallas_call x1, Pallas kernels, per_device(): pl.pallas_call(kernel, out_shape=(pltpu.VMEM((D, PROJ), F32), pltpu.VMEM(...  64.9 us

profile of v8, /device:TPU:1, one launch (start us, length us, event | category | flops | bytes accessed | tf_op | source)
XLA Modules:
  0.0 68.0 jit_solution(812782774283628888)
XLA Ops:
  0.6 64.9 %simclr_head.1 = (f32[4096,128]{1,0:T(8,128)S(1)}, f32[1,1]{1,0:T(1,128)S(1)}) custom-call(bf16[256,4096]{1,0:T(8,128)(2,1)} %f_hbm.1, bf16[4096,128]{1,0:T(8,128)(2,1)} %w_hbm.1, s32[2,128]{1,0:T(2,128)} %bitcast.2), custom_call_target="tpu_custom_call" | custom-call | tf_op jit(solution)/shard_map/simclr_head/pallas_call | solution.py:578
  65.6 1.3 %copy.8 = f32[4096,128]{1,0:T(8,128)} copy(f32[4096,128]{1,0:T(8,128)S(1)} %get-tuple-element.7) | data formatting | bytes 4194304

commit v9 on v8

--- a/solution.py
+++ b/solution.py
@@ -15,7 +15,7 @@
 PROJ = 128
 OWN = 256
 RINGS = 7
-GROUPS = ((RINGS, 11), (11, 14), (14, 16))
+GROUPS = ((RINGS, 11), (11, 16))
 SLOT = OWN + 16
 INV_TAU = 5.0
 SCALE2 = INV_TAU * 1.4426950408889634

time: 68.1 us -> 67.9 us (level)
  no operation moved by 1% of the time
where the time goes in v9:
time: 67.9 us; the launch traced here: 67.8 us
  Pallas kernels  64.6 us (95%)
  between operations  1.8 us (3%)
  local copies, waits for them, and re-layouts  1.32 us (2%)
    pallas_call x1, Pallas kernels, per_device(): pl.pallas_call(kernel, out_shape=(pltpu.VMEM((D, PROJ), F32), pltpu.VMEM(...  64.6 us

profile of v9, /device:TPU:1, one launch (start us, length us, event | category | flops | bytes accessed | tf_op | source)
XLA Modules:
  0.0 67.8 jit_solution(253765666746824419)
XLA Ops:
  0.6 64.6 %simclr_head.1 = (f32[4096,128]{1,0:T(8,128)S(1)}, f32[1,1]{1,0:T(1,128)S(1)}) custom-call(bf16[256,4096]{1,0:T(8,128)(2,1)} %f_hbm.1, bf16[4096,128]{1,0:T(8,128)(2,1)} %w_hbm.1, s32[2,128]{1,0:T(2,128)} %bitcast.2), custom_call_target="tpu_custom_call" | custom-call | tf_op jit(solution)/shard_map/simclr_head/pallas_call | solution.py:578
  65.3 1.3 %copy.8 = f32[4096,128]{1,0:T(8,128)} copy(f32[4096,128]{1,0:T(8,128)S(1)} %get-tuple-element.7) | data formatting | bytes 4194304
